TPU v7x, 32 devices: a whole 2x2x4 slice. The times are simulated.
32 devices in a mesh: grp: 4 (over y, x), batch: 8 (over z, core).
Axes of the slice: x: 2, y: 2, z: 4, core: 2. Of those that a mesh axis runs over, the one named last changes fastest.
Arguments:
- features: bfloat16 [25088, 2048], P('batch', 'grp'), may hold values from -40 to 40
- pixel_mask: int32 [25088], P('batch'), may hold values from 0 to 1, as said below
- out_cotangent: bfloat16 [25088, 2048], P('batch', 'grp'), may hold values from -40 to 40
- reduce_master: float32 [2048, 1024], P(('grp', 'batch')), may hold values from -0.125 to 0.125
- group_master: float32 [288, 1024], P(None, ('grp', 'batch')), may hold values from -0.375 to 0.375
- expand_master: float32 [1024, 2048], P('batch', 'grp'), may hold values from -0.1875 to 0.1875
- norm_params: float32 [4, 1024], P(None, 'grp'), may hold values from -1.5 to 1.5, as said below
- out_params: float32 [2, 2048], P(None, 'grp'), may hold values from -1.5 to 1.5, as said below
- reduce_first: float32 [2048, 1024], P(('grp', 'batch')), may hold values from -0.0007324219 to 0.0007324219
- reduce_second: float32 [2048, 1024], P(('grp', 'batch')), may hold values from 2.2235029e-10 to 8.8940116e-10
- group_first: float32 [288, 1024], P(None, ('grp', 'batch')), may hold values from -0.0007324219 to 0.0007324219
- group_second: float32 [288, 1024], P(None, ('grp', 'batch')), may hold values from 2.2235029e-10 to 8.8940116e-10
- expand_first: float32 [1024, 2048], P('batch', 'grp'), may hold values from -0.0007324219 to 0.0007324219
- expand_second: float32 [1024, 2048], P('batch', 'grp'), may hold values from 2.2235029e-10 to 8.8940116e-10
- norm_first: float32 [4, 1024], P(None, 'grp'), may hold values from -0.0009765625 to 0.0009765625
- norm_second: float32 [4, 1024], P(None, 'grp'), may hold values from 4.4470058e-10 to 1.7788023e-09
- out_first: float32 [2, 2048], P(None, 'grp'), may hold values from -0.0009765625 to 0.0009765625
- out_second: float32 [2, 2048], P(None, 'grp'), may hold values from 4.4470058e-10 to 1.7788023e-09
Outputs:
- block_out: bfloat16 [25088, 2048], P('batch', 'grp')
- input_grad: bfloat16 [25088, 2048], P('batch', 'grp')
- grad_norm: float32 [], replicated
- weight_trust: float32 [3], replicated
- norm_trust: float32 [2], replicated
- reduce_grad: float32 [2048, 1024], P(('grp', 'batch'))
- reduce_first_new: float32 [2048, 1024], P(('grp', 'batch'))
- reduce_second_new: float32 [2048, 1024], P(('grp', 'batch'))
- reduce_new: float32 [2048, 1024], P(('grp', 'batch'))
- reduce_low: bfloat16 [2048, 1024], P(('grp', 'batch'))
- group_grad: float32 [288, 1024], P(None, ('grp', 'batch'))
- group_first_new: float32 [288, 1024], P(None, ('grp', 'batch'))
- group_second_new: float32 [288, 1024], P(None, ('grp', 'batch'))
- group_new: float32 [288, 1024], P(None, ('grp', 'batch'))
- group_low: bfloat16 [288, 1024], P(None, ('grp', 'batch'))
- expand_grad: float32 [1024, 2048], P('batch', 'grp')
- expand_first_new: float32 [1024, 2048], P('batch', 'grp')
- expand_second_new: float32 [1024, 2048], P('batch', 'grp')
- expand_new: float32 [1024, 2048], P('batch', 'grp')
- expand_low: bfloat16 [1024, 2048], P('batch', 'grp')
- norm_grad: float32 [4, 1024], P(None, 'grp')
- norm_first_new: float32 [4, 1024], P(None, 'grp')
- norm_second_new: float32 [4, 1024], P(None, 'grp')
- norm_new: float32 [4, 1024], P(None, 'grp')
- out_grad: float32 [2, 2048], P(None, 'grp')
- out_first_new: float32 [2, 2048], P(None, 'grp')
- out_second_new: float32 [2, 2048], P(None, 'grp')
- out_new: float32 [2, 2048], P(None, 'grp')
Inputs may be any that keep to these rules, and one draw needn't show every extreme that they name: `pixel_mask`: each image's valid pixels form the top-left rectangle of its 7 x 7 frame; one side of the rectangle has 7 pixels, the other 3 to 7. `norm_params`: rows 0 and 2 lie in 0.6 to 1.4. `out_params`: row 0 lies in 0.6 to 1.4.
All inputs are finite; a program needn't handle non-finite values.
Results may differ from a plain program's by a relative error of at most 0.025.
Values may be sent and summed in bfloat16 or wider, within the bound.
A program may use at most 192 MiB of HBM per device.

v0:
```python
import jax
import jax.numpy as jnp
from jax import lax
from jax.sharding import PartitionSpec as P

GW = 32
SIDE = 7


eps_norm = 1e-05
beta_one = 0.9
beta_two = 0.999
adam_eps = 1e-08
learn_rate = 0.25
step_count = 10.0
clip_norm = 1.0


def split_up(value, dim, devices):
    before, after = (value.shape[:dim], value.shape[dim + 1 :])
    return jnp.moveaxis(value.reshape(*before, devices, -1, *after), dim, 0)


def summed_on_arrival(value, axis, dim):
    devices = lax.axis_size(axis)
    pieces = lax.all_to_all(split_up(value, dim, devices), axis, 0, 0, tiled=True)
    return jnp.sum(pieces.astype(jnp.float32), axis=0)


def smooth_act(values):
    return values * jax.nn.sigmoid(values)


def smooth_slope(values):
    sigma = jax.nn.sigmoid(values)
    return sigma * (1.0 + values * (1.0 - sigma))


def matmul_left(first_op, second_op):
    return lax.dot_general(
        first_op, second_op, (((0,), (0,)), ((), ())), preferred_element_type=jnp.float32
    )


def matmul_right(first_op, second_op):
    return lax.dot_general(
        first_op, second_op, (((1,), (1,)), ((), ())), preferred_element_type=jnp.float32
    )


def norm_stats(values, validity):
    weighted = values * validity[:, None]
    count_here = jnp.sum(validity)
    totals, counted = lax.psum((jnp.sum(weighted, axis=0), count_here), "batch")
    centre = totals / counted
    centred = values - centre
    spread = lax.psum(jnp.sum(centred * centred * validity[:, None], axis=0), "batch")
    variance = spread / counted
    scaling = lax.rsqrt(variance + eps_norm)
    return (centred * scaling, scaling, counted)


def norm_back(grad_out, normed, scaling, gain_row, validity, counted):
    bias_grad, gain_grad = lax.psum(
        (jnp.sum(grad_out, axis=0), jnp.sum(grad_out * normed, axis=0)), "batch"
    )
    grad_in = (
        validity[:, None]
        * (gain_row * scaling)
        * (grad_out - (bias_grad + normed * gain_grad) / counted)
    )
    return (grad_in, gain_grad, bias_grad)


def frame_taps(values, reverse):
    channels = values.shape[1]
    images = values.shape[0] // (SIDE * SIDE)
    framed = values.reshape(images, SIDE, SIDE, channels)
    padded = jnp.pad(framed, ((0, 0), (1, 1), (1, 1), (0, 0)))
    pieces = []
    for tap_row in range(3):
        for tap_col in range(3):
            top_edge = 2 - tap_row if reverse else tap_row
            left_edge = 2 - tap_col if reverse else tap_col
            pieces.append(padded[:, top_edge : top_edge + SIDE, left_edge : left_edge + SIDE])
    return jnp.concatenate(pieces, axis=-1).reshape(images * SIDE * SIDE, 9 * channels)


def group_selector(channels):
    owners = jnp.arange(channels) // GW
    return jnp.arange(channels // GW)[:, None] == owners[None, :]


def block_diagonal(weight, selector):
    channels = selector.shape[1]
    tap_rows = weight.reshape(9, 1, GW, channels)
    expanded = jnp.where(selector[None, :, None, :], tap_rows, jnp.zeros((), weight.dtype))
    return expanded.reshape(9 * channels, channels)


def block_extract(product, selector):
    groups_here, channels = selector.shape
    regrouped = product.reshape(9, groups_here, GW, channels)
    return jnp.sum(jnp.where(selector[None, :, None, :], regrouped, 0.0), axis=1).reshape(
        9 * GW, channels
    )


def adam_direction(tensor, clipped, moment_one, moment_two, decay_rate):
    new_first = beta_one * moment_one + (1.0 - beta_one) * clipped
    new_second = beta_two * moment_two + (1.0 - beta_two) * clipped * clipped
    first_hat = new_first / (1.0 - beta_one**step_count)
    second_hat = new_second / (1.0 - beta_two**step_count)
    direction = first_hat / (jnp.sqrt(second_hat) + adam_eps) + decay_rate * tensor
    return (new_first, new_second, direction)


def local(
    features,
    pixel_mask,
    out_cotangent,
    reduce_master,
    group_master,
    expand_master,
    norm_params,
    out_params,
    reduce_first,
    reduce_second,
    group_first,
    group_second,
    expand_first,
    expand_second,
    norm_first,
    norm_second,
    out_first,
    out_second,
):
    validity = pixel_mask.astype(jnp.float32)
    column = validity[:, None]
    reduce_w, group_w, expand_w = (
        lax.all_gather(reduce_master.astype(jnp.bfloat16), "batch", axis=0, tiled=True),
        lax.all_gather(group_master.astype(jnp.bfloat16), "batch", axis=1, tiled=True),
        lax.all_gather(expand_master.astype(jnp.bfloat16), "batch", axis=0, tiled=True),
    )
    own_width = group_w.shape[1]
    z_reduce = lax.psum_scatter(
        jnp.dot(features, reduce_w, preferred_element_type=jnp.float32).astype(jnp.bfloat16),
        "grp",
        scatter_dimension=1,
        tiled=True,
    ).astype(jnp.float32)
    normed_one, scale_one, count_one = norm_stats(z_reduce, validity)
    pre_one = normed_one * norm_params[0] + norm_params[1]
    act_one = (smooth_act(pre_one) * column).astype(jnp.bfloat16)
    selector = group_selector(own_width)
    blocks = block_diagonal(group_w, selector)
    taps_one = frame_taps(act_one, False)
    z_group = jnp.dot(taps_one, blocks, preferred_element_type=jnp.float32)
    normed_two, scale_two, count_two = norm_stats(z_group, validity)
    pre_two = normed_two * norm_params[2] + norm_params[3]
    act_two = (smooth_act(pre_two) * column).astype(jnp.bfloat16)
    act_full = lax.all_gather(act_two, "grp", axis=1, tiled=True)
    z_expand = jnp.dot(act_full, expand_w, preferred_element_type=jnp.float32)
    normed_three, scale_three, count_three = norm_stats(z_expand, validity)
    summed = normed_three * out_params[0] + out_params[1] + features.astype(jnp.float32)
    block_out = (smooth_act(summed) * column).astype(jnp.bfloat16)
    grad_summed = out_cotangent.astype(jnp.float32) * smooth_slope(summed) * column
    grad_three, gain_three, bias_three = norm_back(
        grad_summed, normed_three, scale_three, out_params[0], validity, count_three
    )
    grad_expand = grad_three.astype(jnp.bfloat16)
    expand_raw = matmul_left(act_full, grad_expand)
    grad_act_two = lax.psum_scatter(
        matmul_right(grad_expand, expand_w).astype(jnp.bfloat16),
        "grp",
        scatter_dimension=1,
        tiled=True,
    ).astype(jnp.float32)
    grad_pre_two = grad_act_two * smooth_slope(pre_two) * column
    grad_two, gain_two, bias_two = norm_back(
        grad_pre_two, normed_two, scale_two, norm_params[2], validity, count_two
    )
    grad_group = grad_two.astype(jnp.bfloat16)
    group_raw = block_extract(matmul_left(taps_one, grad_group), selector)
    channels = blocks.shape[1]
    turned = (
        blocks.reshape(9, channels, channels).transpose(0, 2, 1).reshape(9 * channels, channels)
    )
    grad_act_one = jnp.dot(frame_taps(grad_group, True), turned, preferred_element_type=jnp.float32)
    grad_pre_one = grad_act_one * smooth_slope(pre_one) * column
    grad_one, gain_one, bias_one = norm_back(
        grad_pre_one, normed_one, scale_one, norm_params[0], validity, count_one
    )
    grad_reduce = lax.all_gather(grad_one.astype(jnp.bfloat16), "grp", axis=1, tiled=True)
    input_grad = (grad_summed + matmul_right(grad_reduce, reduce_w)).astype(jnp.bfloat16)
    reduce_raw = matmul_left(features, grad_reduce)
    reduce_part, group_part, expand_part = (
        summed_on_arrival(reduce_raw.astype(jnp.bfloat16), "batch", 0),
        summed_on_arrival(group_raw.astype(jnp.bfloat16), "batch", 1),
        summed_on_arrival(expand_raw.astype(jnp.bfloat16), "batch", 0),
    )
    norm_raw = jnp.stack([gain_one, bias_one, gain_two, bias_two])
    out_raw = jnp.stack([gain_three, bias_three])
    batch_share = 1.0 / lax.axis_size("batch")
    square_here = (
        jnp.sum(reduce_part * reduce_part)
        + jnp.sum(group_part * group_part)
        + jnp.sum(expand_part * expand_part)
        + batch_share * (jnp.sum(norm_raw * norm_raw) + jnp.sum(out_raw * out_raw))
    )
    grad_norm = jnp.sqrt(lax.psum(square_here, ("grp", "batch")))
    factor = jnp.minimum(1.0, clip_norm / grad_norm)
    tensors = (reduce_master, group_master, expand_master, norm_params, out_params)
    raw_grads = (reduce_part, group_part, expand_part, norm_raw, out_raw)
    moments_one = (reduce_first, group_first, expand_first, norm_first, out_first)
    moments_two = (reduce_second, group_second, expand_second, norm_second, out_second)
    decays = (0.01, 0.01, 0.01, 0.0, 0.0)
    weightings = (1.0, 1.0, 1.0, batch_share, batch_share)
    results = []
    weight_sq = []
    step_sq = []
    for tensor, raw_grad, moment_one, moment_two, decay_rate, weighting in zip(
        tensors, raw_grads, moments_one, moments_two, decays, weightings
    ):
        clipped = factor * raw_grad
        new_first, new_second, direction = adam_direction(
            tensor, clipped, moment_one, moment_two, decay_rate
        )
        results.append((clipped, new_first, new_second, direction))
        weight_sq.append(weighting * jnp.sum(tensor * tensor))
        step_sq.append(weighting * jnp.sum(direction * direction))
    weight_total, step_total = lax.psum(
        (jnp.stack(weight_sq), jnp.stack(step_sq)), ("grp", "batch")
    )
    trust_ratios = jnp.sqrt(weight_total) * lax.rsqrt(step_total + 1e-06)
    updated = []
    for number in range(5):
        updated.append(tensors[number] - learn_rate * trust_ratios[number] * results[number][3])
    return (
        block_out,
        input_grad,
        grad_norm,
        trust_ratios[:3],
        trust_ratios[3:],
        results[0][0],
        results[0][1],
        results[0][2],
        updated[0],
        updated[0].astype(jnp.bfloat16),
        results[1][0],
        results[1][1],
        results[1][2],
        updated[1],
        updated[1].astype(jnp.bfloat16),
        results[2][0],
        results[2][1],
        results[2][2],
        updated[2],
        updated[2].astype(jnp.bfloat16),
        results[3][0],
        results[3][1],
        results[3][2],
        updated[3],
        results[4][0],
        results[4][1],
        results[4][2],
        updated[4],
    )


def solution(mesh):
    in_specs = (
        P("batch", "grp"),
        P("batch"),
        P("batch", "grp"),
        P(("grp", "batch"), None),
        P(None, ("grp", "batch")),
        P("batch", "grp"),
        P(None, "grp"),
        P(None, "grp"),
        P(("grp", "batch"), None),
        P(("grp", "batch"), None),
        P(None, ("grp", "batch")),
        P(None, ("grp", "batch")),
        P("batch", "grp"),
        P("batch", "grp"),
        P(None, "grp"),
        P(None, "grp"),
        P(None, "grp"),
        P(None, "grp"),
    )
    out_specs = (
        P("batch", "grp"),
        P("batch", "grp"),
        P(),
        P(),
        P(),
        P(("grp", "batch"), None),
        P(("grp", "batch"), None),
        P(("grp", "batch"), None),
        P(("grp", "batch"), None),
        P(("grp", "batch"), None),
        P(None, ("grp", "batch")),
        P(None, ("grp", "batch")),
        P(None, ("grp", "batch")),
        P(None, ("grp", "batch")),
        P(None, ("grp", "batch")),
        P("batch", "grp"),
        P("batch", "grp"),
        P("batch", "grp"),
        P("batch", "grp"),
        P("batch", "grp"),
        P(None, "grp"),
        P(None, "grp"),
        P(None, "grp"),
        P(None, "grp"),
        P(None, "grp"),
        P(None, "grp"),
        P(None, "grp"),
        P(None, "grp"),
    )
    return jax.shard_map(local, mesh=mesh, in_specs=in_specs, out_specs=out_specs, check_vma=False)
```

profile of v0, /device:TPU:0, one launch (start us, length us, event | category | flops | bytes accessed | tf_op | source)
XLA Modules:
  0.0 808.3 jit_solution(1687816567990184895)
XLA Ops:
  8.9 26.1 %all-gather.5.cloned.1.call-done = bf16[512,1024]{1,0:T(8,128)(2,1)} async-done(((bf16[64,1024]{1,0:T(8,128)(2,1)}), bf16[512,1024]{1,0:T(8,128)(2,1)}) %all-gather.5.cloned.1.call-update) | async-done | bytes 1048592 | tf_op jit(solution)/shard_map/all_gather | solution.py:141
  35.0 8.4 %convolution_convert_fusion.1 = bf16[3136,1024]{1,0:T(8,128)(2,1)} fusion(bf16[3136,512]{1,0:T(8,128)(2,1)} %param.18, bf16[512,1024]{1,0:T(8,128)(2,1)} %all-gather.5.cloned.1.call-done), kind=kOutput, calls=%fused_computation.17 | convolution fusion | flops 3291545600 | bytes 10682368 | tf_op jit(solution)/shard_map/dot_general | solution.py:147
  46.4 14.1 %all_gather.16 = bf16[288,256]{0,1:T(8,128)(2,1)S(1)} all-gather(bf16[288,32]{0,1:T(8,128)(2,1)S(1)} %convert_element_type.93), channel_id=1, replica_groups=mesh['grp'=4,'batch'=8] {'batch'}, dimensions={1}, use_global_device_ids=true | all-gather | bytes 165888 | tf_op jit(solution)/shard_map/all_gather | solution.py:142
  61.8 52.8 %reduce-scatter.3.cloned.1.call-done = bf16[3136,256]{1,0:T(8,128)(2,1)} async-done(((bf16[3136,1024]{1,0:T(8,128)(2,1)}), bf16[3136,256]{1,0:T(8,128)(2,1)}) %reduce-scatter.3.cloned.1.call-update) | async-done | bytes 1605648 | tf_op jit(solution)/shard_map/reduce_scatter | solution.py:146
  116.6 17.1 %all-reduce.6 = (f32[256]{0:T(256)S(1)}, f32[]{:T(128)}) all-reduce(f32[256]{0:T(256)S(1)} %fusion.24, f32[]{:T(128)} %convert_reduce_fusion.3), channel_id=1, replica_groups=mesh['grp'=4,'batch'=8] {'batch'}, use_global_device_ids=true, to_apply=%region_2.0 | all-reduce | flops 257 | bytes 2056 | tf_op jit(solution)/shard_map/psum | solution.py:54
  136.4 13.8 %psum.120 = f32[256]{0:T(256)S(1)} all-reduce(f32[256]{0:T(256)S(1)} %fusion.23), channel_id=1, replica_groups=mesh['grp'=4,'batch'=8] {'batch'}, use_global_device_ids=true, to_apply=%region_6.0 | all-reduce | flops 256 | bytes 2048 | tf_op jit(solution)/shard_map/psum | solution.py:57
  155.3 11.5 %pad_slice_fusion.8 = (bf16[64,7,7,256]{3,2,1,0:T(8,128)(2,1)}, bf16[64,7,7,256]{3,2,1,0:T(8,128)(2,1)}, bf16[64,7,7,256]{3,2,1,0:T(8,128)(2,1)}, bf16[64,7,7,25...) fusion(bf16[64,7,7,256]{3,2,1,0:T(8,128)(2,1)} %reshape.167), kind=kLoop, calls=%fused_computation.8 | loop fusion | bytes 14450688 | tf_op jit(solution)/shard_map/slice | solution.py:85
  173.0 3.7 concatenate.42
  176.7 3.7 concatenate.43
  180.4 3.8 concatenate.44
  184.2 3.7 concatenate.45
  187.9 3.7 concatenate.46
  203.5 4.3 multiply_reduce_fusion.5
  207.9 14.2 %psum.121 = f32[256]{0:T(256)} all-reduce(f32[256]{0:T(256)S(1)} %get-tuple-element.141), channel_id=1, replica_groups=mesh['grp'=4,'batch'=8] {'batch'}, use_global_device_ids=true, to_apply=%region_8.9 | all-reduce | flops 256 | bytes 2048 | tf_op jit(solution)/shard_map/psum | solution.py:54
  224.4 14.7 %psum.122 = f32[256]{0:T(256)} all-reduce(f32[256]{0:T(256)} %multiply_reduce_fusion.4), channel_id=1, replica_groups=mesh['grp'=4,'batch'=8] {'batch'}, use_global_device_ids=true, to_apply=%region_10.11 | all-reduce | flops 256 | bytes 2048 | tf_op jit(solution)/shard_map/psum | solution.py:57
  245.4 67.8 %all-gather.7.cloned.1.call-done = bf16[3136,1024]{1,0:T(8,128)(2,1)} async-done(((bf16[3136,256]{1,0:T(8,128)(2,1)}), bf16[3136,1024]{1,0:T(8,128)(2,1)}) %all-gather.7.cloned.1.call-update) | async-done | bytes 6422544 | tf_op jit(solution)/shard_map/all_gather | solution.py:162
  313.2 9.3 %multiply_reduce_fusion.2 = (f32[512]{0:T(512)S(1)}, f32[3136,512]{1,0:T(8,128)}) fusion(f32[3136]{0:T(1024)S(1)} %convert_element_type.91, bf16[3136,1024]{1,0:T(8,128)(2,1)} %all-gather.7.cloned.1.call-done, bf16[1024,512]{1,0:T(8,128)(2,1)} %all-gather.9.cloned.1.call-done), kind=kOutput, calls=%fused_computation.26 | convolution fusion | flops 3291545088 | bytes 13908224 | tf_op jit(solution)/shard_map/dot_general | solution.py:163
  322.5 16.9 %psum.123 = f32[512]{0:T(512)} all-reduce(f32[512]{0:T(512)S(1)} %get-tuple-element.143), channel_id=1, replica_groups=mesh['grp'=4,'batch'=8] {'batch'}, use_global_device_ids=true, to_apply=%region_12.13 | all-reduce | flops 512 | bytes 4096 | tf_op jit(solution)/shard_map/psum | solution.py:54
  340.7 4.2 multiply_reduce_fusion.1
  344.9 14.3 %psum.124 = f32[512]{0:T(512)} all-reduce(f32[512]{0:T(512)} %multiply_reduce_fusion.1), channel_id=1, replica_groups=mesh['grp'=4,'batch'=8] {'batch'}, use_global_device_ids=true, to_apply=%region_14.15 | all-reduce | flops 512 | bytes 4096 | tf_op jit(solution)/shard_map/psum | solution.py:57
  361.1 12.5 %fusion.35 = (f32[512]{0:T(512)}, f32[512]{0:T(512)}, f32[3136,512]{1,0:T(8,128)}, bf16[3136,512]{1,0:T(8,128)(2,1)}) fusion(f32[512]{0:T(512)S(1)} %get-tuple-element.109, f32[3136,512]{1,0:T(8,128)} %get-tuple-element.144, f32[512]{0:T(512)S(1)} %broadcast_divide_fusion, f32[3136]{0:T(1024)S(1)} %convert_element_type.91, bf16[3136,512]{1,0:T(8,128)(2,1)} %param.18, ...), kind=kLoop, calls=%fused_computation.154 | loop fusion | flops 35322880 | bytes 22503680 | tf_op jit(solution)/shard_map/reduce_sum | solution.py:65
  373.6 14.3 %all-reduce.5 = (f32[512]{0:T(512)}, f32[512]{0:T(512)}) all-reduce(f32[512]{0:T(512)} %get-tuple-element.57, f32[512]{0:T(512)} %get-tuple-element.56), channel_id=1, replica_groups=mesh['grp'=4,'batch'=8] {'batch'}, use_global_device_ids=true, to_apply=%region_18.19 | all-reduce | flops 1024 | bytes 8192 | tf_op jit(solution)/shard_map/psum | solution.py:64
  387.9 6.6 multiply_convert_fusion
  396.1 5.8 convolution_convert_fusion
  411.8 58.8 %reduce-scatter.5.cloned.1.call-done = bf16[3136,256]{1,0:T(8,128)(2,1)} async-done(((bf16[3136,1024]{1,0:T(8,128)(2,1)}), bf16[3136,256]{1,0:T(8,128)(2,1)}) %reduce-scatter.5.cloned.1.call-update) | async-done | bytes 1605648 | tf_op jit(solution)/shard_map/reduce_scatter | solution.py:173
  470.6 5.2 fusion.37
  475.8 17.2 %all-reduce.4 = (f32[256]{0:T(256)}, f32[256]{0:T(256)}) all-reduce(f32[256]{0:T(256)} %get-tuple-element.61, f32[256]{0:T(256)} %get-tuple-element.60), channel_id=1, replica_groups=mesh['grp'=4,'batch'=8] {'batch'}, use_global_device_ids=true, to_apply=%region_23.24 | all-reduce | flops 512 | bytes 4096 | tf_op jit(solution)/shard_map/psum | solution.py:64
  493.0 4.4 multiply_convert_fusion.2
  501.1 10.8 %pad_slice_fusion = (bf16[64,7,7,256]{3,2,1,0:T(8,128)(2,1)}, bf16[64,7,7,256]{3,2,1,0:T(8,128)(2,1)}, bf16[64,7,7,256]{3,2,1,0:T(8,128)(2,1)}, bf16[64,7,7,256]...) fusion(bf16[64,7,7,256]{3,2,1,0:T(8,128)(2,1)} %reshape.168), kind=kLoop, calls=%fused_computation | loop fusion | bytes 14450688 | tf_op jit(solution)/shard_map/slice | solution.py:85
  511.9 3.8 concatenate.56
  515.6 3.8 concatenate.50
  523.1 3.7 concatenate.52
  530.4 3.7 concatenate.54
  534.2 3.7 concatenate.55
  547.7 7.9 fusion.36
  555.6 14.5 %all-reduce.3 = (f32[256]{0:T(256)}, f32[256]{0:T(256)}) all-reduce(f32[256]{0:T(256)} %get-tuple-element.59, f32[256]{0:T(256)} %get-tuple-element.58), channel_id=1, replica_groups=mesh['grp'=4,'batch'=8] {'batch'}, use_global_device_ids=true, to_apply=%region_27.28 | all-reduce | flops 512 | bytes 4096 | tf_op jit(solution)/shard_map/psum | solution.py:64
  570.1 4.5 fusion.25
  574.6 8.5 %convolution_convert_fusion.2 = bf16[1024,512]{1,0:T(8,128)(2,1)} fusion(bf16[3136,1024]{1,0:T(8,128)(2,1)} %all-gather.7.cloned.1.call-done, bf16[3136,512]{1,0:T(8,128)(2,1)} %copy-done.17), kind=kOutput, calls=%fused_computation.71 | convolution fusion | flops 3288858624 | bytes 10682368 | tf_op jit(solution)/shard_map/dot_general | solution.py:40
  586.6 19.4 %copy.74 = bf16[2304,3136]{1,0:T(8,128)(2,1)} copy(bf16[2304,3136]{0,1:T(8,128)(2,1)} %bitcast.66) | data formatting | bytes 28901376 | tf_op jit(solution)/shard_map/dot_general | solution.py:40
  606.0 10.7 %select_reduce_fusion = bf16[9,32,256]{2,1,0:T(8,128)(2,1)} fusion(pred[8,256]{1,0:T(8,128)(4,1)S(1)} %copy-done.38, bf16[9,8,32,3136]{3,2,1,0:T(8,128)(2,1)} %bitcast.67, bf16[3136,256]{1,0:T(8,128)(2,1)S(1)} %copy-done.3), kind=kOutput, calls=%fused_computation.66 | convolution fusion | flops 3700482048 | bytes 16205824 | tf_op jit(solution)/shard_map/dot_general | solution.py:40
  619.0 5.3 all-to-all-start.1
  624.3 18.8 %all-gather.11.cloned.1.call-done = bf16[3136,1024]{1,0:T(8,128)(2,1)} async-done(((bf16[3136,256]{1,0:T(8,128)(2,1)}), bf16[3136,1024]{1,0:T(8,128)(2,1)}) %all-gather.11.cloned.1.call-update) | async-done | bytes 6422544 | tf_op jit(solution)/shard_map/all_gather | solution.py:194
  643.1 8.4 %convolution_convert_fusion.3 = bf16[1024,512]{0,1:T(8,128)(2,1)} fusion(bf16[3136,1024]{1,0:T(8,128)(2,1)} %all-gather.11.cloned.1.call-done, bf16[3136,512]{1,0:T(8,128)(2,1)} %param.18), kind=kOutput, calls=%fused_computation.72 | convolution fusion | flops 3288858624 | bytes 10682368 | tf_op jit(solution)/shard_map/dot_general | solution.py:40
  651.6 4.7 all-to-all-start
  660.5 22.4 %all-to-all-done = bf16[8,64,1024]{2,1,0:T(8,128)(2,1)S(1)} async-done(((bf16[8,64,1024]{2,1,0:T(8,128)(2,1)}), bf16[8,64,1024]{2,1,0:T(8,128)(2,1)S(1)}, u32[]{:S(2)}, u32[]{:S(2)}) %all-to-all-start) | async-done | bytes 1048608 | tf_op jit(solution)/shard_map/all_to_all | solution.py:26
  685.7 36.9 %psum.131 = f32[]{:T(128)} all-reduce(f32[]{:T(128)S(6)} %add.260), channel_id=1, replica_groups=mesh['grp'=4,'batch'=8] {'grp','batch'}, use_global_device_ids=true, to_apply=%region_37.38 | all-reduce | flops 1 | bytes 8 | tf_op jit(solution)/shard_map/psum | solution.py:211
  739.1 10.2 %add_convert_fusion = bf16[3136,512]{1,0:T(8,128)(2,1)} fusion(f32[3136,512]{1,0:T(8,128)} %get-tuple-element.110, bf16[3136,1024]{1,0:T(8,128)(2,1)} %all-gather.11.cloned.1.call-done, bf16[512,1024]{1,0:T(8,128)(2,1)} %all-gather.5.cloned.1.call-done), kind=kOutput, calls=%fused_computation.18 | convolution fusion | flops 3291545600 | bytes 17104896 | tf_op jit(solution)/shard_map/dot_general | solution.py:46
  749.3 42.5 %all-reduce.2 = (f32[5]{0:T(128)S(1)}, f32[5]{0:T(128)S(1)}) all-reduce(f32[5]{0:T(128)S(1)} %stack.61, f32[5]{0:T(128)S(1)} %stack.55), channel_id=1, replica_groups=mesh['grp'=4,'batch'=8] {'grp','batch'}, use_global_device_ids=true, to_apply=%region_49.50 | all-reduce | flops 10 | bytes 80 | tf_op jit(solution)/shard_map/psum | solution.py:232
  (217 shorter events, 105.4 us)
Async XLA Ops:
  7.2 27.8 %all-gather.5.cloned.1.call-start = ((), (), s32[]{:S(2)}) async-start(), calls=%async_computation.5 | async-start | bytes 1179648 | tf_op jit(solution)/shard_map/all_gather | solution.py:141
  8.9 105.7 %reduce-scatter.3.cloned.1.call-start = ((), (), s32[]{:S(2)}) async-start(), calls=%async_computation.6 | async-start | bytes 8028160 | tf_op jit(solution)/shard_map/reduce_scatter | solution.py:146
  43.4 2.3 copy-start.34
  43.4 2.9 copy-start.27
  43.5 201.9 %all-gather.9.cloned.1.call-start = ((), (), s32[]{:S(2)}) async-start(), calls=%async_computation.8 | async-start | bytes 1179648 | tf_op jit(solution)/shard_map/all_gather | solution.py:143
  45.1 268.1 %all-gather.7.cloned.1.call-start = ((), (), s32[]{:S(2)}) async-start(), calls=%async_computation.7 | async-start | bytes 8028160 | tf_op jit(solution)/shard_map/all_gather | solution.py:162
  45.8 108.0 %copy-start.37 = (pred[8,256]{1,0:T(8,128)(4,1)}, pred[8,256]{1,0:T(8,128)(4,1)S(1)}, u32[]{:S(2)}) copy-start(pred[8,256]{1,0:T(8,128)(4,1)S(1)} %iota_compare_fusion) | copy-start | bytes 6148
  46.4 105.0 %copy-start.44 = (f32[1,256]{1,0:T(1,128)}, f32[1,256]{1,0:T(1,128)S(1)}, u32[]{:S(2)}) copy-start(f32[1,256]{1,0:T(1,128)S(1)} %get-tuple-element.133) | copy-start | bytes 3076
  114.6 36.8 %copy-start = (bf16[3136,256]{1,0:T(8,128)(2,1)S(1)}, bf16[3136,256]{1,0:T(8,128)(2,1)}, u32[]{:S(2)}) copy-start(bf16[3136,256]{1,0:T(8,128)(2,1)} %reduce-scatter.3.cloned.1.call-done) | copy-start | bytes 4816900
  151.4 47.4 %copy-start.42 = (f32[256]{0:T(256)}, f32[256]{0:T(256)S(1)}, u32[]{:S(2)}) copy-start(f32[256]{0:T(256)S(1)} %get-tuple-element.104) | copy-start | bytes 3076
  195.3 1.9 copy-start.15
  195.3 2.4 copy-start.13
  202.2 5.7 copy-start.2
  207.9 31.2 %copy-start.48 = (f32[1,256]{1,0:T(1,128)S(1)}, f32[1,256]{1,0:T(1,128)}, u32[]{:S(2)}) copy-start(f32[1,256]{1,0:T(1,128)} %get-tuple-element.130) | copy-start | bytes 3076
  223.4 21.3 %copy-start.35 = (f32[256]{0:T(256)}, f32[256]{0:T(256)S(1)}, u32[]{:S(2)}) copy-start(f32[256]{0:T(256)S(1)} %broadcast_divide_fusion.1) | copy-start | bytes 3076
  241.6 3.2 copy-start.33
  244.7 225.9 %reduce-scatter.5.cloned.1.call-start = ((), (), s32[]{:S(2)}) async-start(), calls=%async_computation.9 | async-start | bytes 8028160 | tf_op jit(solution)/shard_map/reduce_scatter | solution.py:173
  361.1 12.5 %copy-start.39 = (f32[512]{0:T(512)}, f32[512]{0:T(512)S(1)}, u32[]{:S(2)}) copy-start(f32[512]{0:T(512)S(1)} %get-tuple-element.109) | copy-start | bytes 6148
  387.9 8.3 %copy-start.60 = (bf16[1024,512]{1,0:T(8,128)(2,1)S(1)}, bf16[1024,512]{1,0:T(8,128)(2,1)}, u32[]{:S(2)}) copy-start(bf16[1024,512]{1,0:T(8,128)(2,1)} %all-gather.9.cloned.1.call-done) | copy-start | bytes 3145732
  401.9 68.7 %copy-start.36 = (f32[256]{0:T(256)S(1)}, f32[256]{0:T(256)}, u32[]{:S(2)}) copy-start(f32[256]{0:T(256)} %copy-done.35) | copy-start | bytes 3076
  401.9 241.1 %all-gather.11.cloned.1.call-start = ((), (), s32[]{:S(2)}) async-start(), calls=%async_computation.10 | async-start | bytes 8028160 | tf_op jit(solution)/shard_map/all_gather | solution.py:194
  539.3 1.9 copy-start.16
  539.3 2.4 copy-start.14
  545.8 1.9 copy-start.46
  583.0 35.9 %all-to-all-start.2 = ((bf16[8,128,512]{2,1,0:T(8,128)(2,1)}), bf16[8,128,512]{2,1,0:T(8,128)(2,1)S(1)}, u32[]{:S(2)}, u32[]{:S(2)}) async-start(bf16[8,128,512]{2,1,0:T(8,128)(2,1)} %bitcast.74), calls=%async_computation.4 | async-start | bytes 2097152 | tf_op jit(solution)/shard_map/all_to_all | solution.py:26
  586.6 19.4 %copy-start.38 = (pred[8,256]{1,0:T(8,128)(4,1)S(1)}, pred[8,256]{1,0:T(8,128)(4,1)}, u32[]{:S(2)}) copy-start(pred[8,256]{1,0:T(8,128)(4,1)} %copy-done.37) | copy-start | bytes 6148
  619.0 32.6 %all-to-all-start.1 = ((bf16[8,288,32]{1,2,0:T(8,128)(2,1)}), bf16[8,288,32]{1,2,0:T(8,128)(2,1)S(1)}, u32[]{:S(2)}, u32[]{:S(2)}) async-start(bf16[8,288,32]{1,2,0:T(8,128)(2,1)} %copy.75), calls=%async_computation.3 | async-start | bytes 393216 | tf_op jit(solution)/shard_map/all_to_all | solution.py:26
  624.3 32.1 %copy-start.40 = (f32[512]{0:T(512)S(1)}, f32[512]{0:T(512)}, u32[]{:S(2)}) copy-start(f32[512]{0:T(512)} %get-tuple-element.74) | copy-start | bytes 6148
  624.3 32.1 %copy-start.41 = (f32[512]{0:T(512)S(1)}, f32[512]{0:T(512)}, u32[]{:S(2)}) copy-start(f32[512]{0:T(512)} %get-tuple-element.75) | copy-start | bytes 6148
  651.5 6.3 copy-start.52
  651.5 6.3 copy-start.53
  651.5 6.3 copy-start.54
  651.5 6.3 copy-start.55
  651.5 71.9 %copy-start.56 = (f32[2,512]{1,0:T(2,128)S(1)}, f32[2,512]{1,0:T(2,128)}, u32[]{:S(2)}) copy-start(f32[2,512]{1,0:T(2,128)} %param.34) | copy-start | bytes 12292
  651.5 71.9 %copy-start.57 = (f32[2,512]{1,0:T(2,128)S(1)}, f32[2,512]{1,0:T(2,128)}, u32[]{:S(2)}) copy-start(f32[2,512]{1,0:T(2,128)} %param.35) | copy-start | bytes 12292
  651.5 74.4 %copy-start.58 = (f32[4,256]{1,0:T(4,128)S(1)}, f32[4,256]{1,0:T(4,128)}, u32[]{:S(2)}) copy-start(f32[4,256]{1,0:T(4,128)} %param.32) | copy-start | bytes 12292
  651.6 74.4 %copy-start.59 = (f32[4,256]{1,0:T(4,128)S(1)}, f32[4,256]{1,0:T(4,128)}, u32[]{:S(2)}) copy-start(f32[4,256]{1,0:T(4,128)} %param.33) | copy-start | bytes 12292
  651.6 76.9 %copy-start.31 = (f32[288,32]{0,1:T(8,128)S(1)}, f32[288,32]{0,1:T(8,128)}, u32[]{:S(2)}) copy-start(f32[288,32]{0,1:T(8,128)} %param.28) | copy-start | bytes 110596
  651.6 76.9 %copy-start.32 = (f32[288,32]{0,1:T(8,128)S(1)}, f32[288,32]{0,1:T(8,128)}, u32[]{:S(2)}) copy-start(f32[288,32]{0,1:T(8,128)} %param.29) | copy-start | bytes 110596
  651.6 31.3 %all-to-all-start = ((bf16[8,64,1024]{2,1,0:T(8,128)(2,1)}), bf16[8,64,1024]{2,1,0:T(8,128)(2,1)S(1)}, u32[]{:S(2)}, u32[]{:S(2)}) async-start(bf16[8,64,1024]{2,1,0:T(8,128)(2,1)} %bitcast.13), calls=%async_computation.2 | async-start | bytes 2097152 | tf_op jit(solution)/shard_map/all_to_all | solution.py:26
  656.4 76.0 %copy-start.19 = (f32[64,1024]{1,0:T(8,128)S(1)}, f32[64,1024]{1,0:T(8,128)}, u32[]{:S(2)}) copy-start(f32[64,1024]{1,0:T(8,128)} %param.21) | copy-start | bytes 786436
  729.7 67.7 %copy-start.28 = (f32[288,32]{0,1:T(8,128)}, f32[288,32]{0,1:T(8,128)S(1)}, u32[]{:S(2)}) copy-start(f32[288,32]{0,1:T(8,128)S(1)} %get-tuple-element.97) | copy-start | bytes 110596
  729.7 67.7 %copy-start.29 = (f32[288,32]{0,1:T(8,128)}, f32[288,32]{0,1:T(8,128)S(1)}, u32[]{:S(2)}) copy-start(f32[288,32]{0,1:T(8,128)S(1)} %get-tuple-element.98) | copy-start | bytes 110596
  732.3 65.8 %copy-start.23 = (f32[128,512]{1,0:T(8,128)}, f32[128,512]{1,0:T(8,128)S(1)}, u32[]{:S(2)}) copy-start(f32[128,512]{1,0:T(8,128)S(1)} %get-tuple-element.94) | copy-start | bytes 786436
  732.3 65.8 %copy-start.24 = (f32[128,512]{1,0:T(8,128)}, f32[128,512]{1,0:T(8,128)S(1)}, u32[]{:S(2)}) copy-start(f32[128,512]{1,0:T(8,128)S(1)} %get-tuple-element.95) | copy-start | bytes 786436
  735.1 63.9 %copy-start.25 = (f32[64,1024]{1,0:T(8,128)}, f32[64,1024]{1,0:T(8,128)S(1)}, u32[]{:S(2)}) copy-start(f32[64,1024]{1,0:T(8,128)S(1)} %get-tuple-element.100) | copy-start | bytes 786436
  735.1 63.9 %copy-start.26 = (f32[64,1024]{1,0:T(8,128)}, f32[64,1024]{1,0:T(8,128)S(1)}, u32[]{:S(2)}) copy-start(f32[64,1024]{1,0:T(8,128)S(1)} %get-tuple-element.101) | copy-start | bytes 786436
  791.8 8.1 %copy-start.49 = (f32[5]{0:T(128)}, f32[5]{0:T(128)S(1)}, u32[]{:S(2)}) copy-start(f32[5]{0:T(128)S(1)} %rsqrt_multiply_fusion) | copy-start | bytes 64
  (22 other events, 32.9 us)
Sparse Core Ops, SparseCore 0:
  10.2 24.7 all-gather.4
  43.6 70.9 reduce-scatter.2
  116.7 22.1 all-gather.8
  244.8 68.3 all-gather.6
  402.0 68.5 reduce-scatter.4
  574.7 68.3 all-gather.10
where the time goes:
time: 816 us; the launch traced here: 808 us
  waiting for transfers between devices  247 us (30%)
  blocking collectives  230 us (28%)
  local copies, waits for them, and re-layouts  137 us (17%)
  other arithmetic  80.6 us (10%)
  matrix products  73.4 us (9%)
  between operations  26.1 us (3%)
  starting transfers between devices  13.9 us (2%)
    all_gather x1, waiting for transfers between devices, local(): act_full = lax.all_gather(act_two, 'grp', axis=1, tiled=True)  67.8 us
    reduce_scatter x1, waiting for transfers between devices, local(): lax.psum_scatter(matmul_right(grad_expand, expand_w).astype(jnp.bfloat16)...  58.8 us
    concatenate x18, local copies, waits for them, and re-layouts, frame_taps(): jnp.concatenate(pieces, axis=-1).reshape(images * SIDE * SIDE, 9 * channels)  56.2 us
    reduce_scatter x1, waiting for transfers between devices, local(): lax.psum_scatter(jnp.dot(features, reduce_w, preferred_element_type=jnp.f...  52.8 us
    psum x3, blocking collectives, norm_stats(): totals, counted = lax.psum((jnp.sum(weighted, axis=0), count_here), 'batch')  48.2 us
    psum x3, blocking collectives, norm_back(): lax.psum((jnp.sum(grad_out, axis=0), jnp.sum(grad_out * normed, axis=0)),...  46 us
    psum x3, blocking collectives, norm_stats(): lax.psum(jnp.sum(centred * centred * validity[:, None], axis=0), 'batch')  42.8 us
    psum x1, blocking collectives, local(): lax.psum((jnp.stack(weight_sq), jnp.stack(step_sq)), ('grp', 'batch'))  42.5 us
  transfers between devices with their start and end apart: 9, of which 6 were waited for; matrix products, arithmetic and copies ran while one was open for 16% of the time, Pallas kernels for 0%

commit v1 on v0

v1 whole, which is shorter than its diff:
```python
import functools

import jax
import jax.numpy as jnp
from jax import lax
from jax.experimental import pallas as pl
from jax.experimental.pallas import tpu as pltpu
from jax.sharding import PartitionSpec as P

GW = 32
SIDE = 7
HW = SIDE * SIDE
BLK = 256

eps_norm = 1e-05
beta_one = 0.9
beta_two = 0.999
adam_eps = 1e-08
learn_rate = 0.25
step_count = 10.0
clip_norm = 1.0

MESH = pl.DeviceIdType.MESH
F32 = jnp.float32
BF16 = jnp.bfloat16
VMEM_LIMIT = 60 * 1024 * 1024


def params(**more):
    return pltpu.CompilerParams(vmem_limit_bytes=VMEM_LIMIT, **more)


def dot(a, b):
    return jnp.dot(a, b, preferred_element_type=F32)


def dot_left(a, b):
    return lax.dot_general(a, b, (((0,), (0,)), ((), ())), preferred_element_type=F32)


def dot_right(a, b):
    return lax.dot_general(a, b, (((1,), (1,)), ((), ())), preferred_element_type=F32)


def sigmoid(v):
    return 0.5 + 0.5 * jnp.tanh(0.5 * v)


def to_inner(rows, images):
    to = lax.broadcasted_iota(jnp.int32, (rows, rows), 0)
    source = (to % images) * HW + to // images
    at = lax.broadcasted_iota(jnp.int32, (rows, rows), 1)
    return jnp.where(at == source, 1.0, 0.0).astype(BF16)


def to_outer(rows, images):
    to = lax.broadcasted_iota(jnp.int32, (rows, rows), 0)
    source = (to % HW) * images + to // HW
    at = lax.broadcasted_iota(jnp.int32, (rows, rows), 1)
    return jnp.where(at == source, 1.0, 0.0).astype(BF16)


def wide(mask, columns):
    return jnp.concatenate([mask] * (columns // 128), axis=1)


def peers(axis):
    size = lax.axis_size(axis)
    mine = lax.axis_index(axis)
    return [{axis: lax.rem(mine + other, size)} for other in range(1, size)]


def greet(groups):
    barrier = pltpu.get_barrier_semaphore()
    for peer in groups:
        pl.semaphore_signal(barrier, inc=1, device_id=peer, device_id_type=MESH)


def greeted(groups):
    pl.semaphore_wait(pltpu.get_barrier_semaphore(), len(groups))


def everyone():
    return peers("grp") + peers("batch")


def sums_scratch(rows, columns):
    grp, batch = lax.axis_size("grp"), lax.axis_size("batch")
    return [
        pltpu.VMEM((grp - 1, rows, columns), F32),
        pltpu.VMEM((batch - 1, rows, columns), F32),
        pltpu.VMEM((rows, columns), F32),
        pltpu.SemaphoreType.DMA((grp - 1,)),
        pltpu.SemaphoreType.DMA((grp - 1,)),
        pltpu.SemaphoreType.DMA((batch - 1,)),
        pltpu.SemaphoreType.DMA((batch - 1,)),
    ]


def add_rows(parts):
    return functools.reduce(jnp.add, parts)


def merge_stats(parts):
    count = add_rows([part[2:3] for part in parts])
    total = add_rows([part[0:1] for part in parts])
    centre = total / count
    spread = add_rows([part[1:2] + part[2:3] * (part[0:1] / part[2:3] - centre) ** 2 for part in parts])
    return jnp.concatenate([total, spread, count], axis=0)


def over_devices(source, scratch, merge):
    first, second, mid, *sems = scratch
    copies = []
    for axis, slots, send, recv in (("grp", first, sems[0], sems[1]), ("batch", second, sems[2], sems[3])):
        here = []
        for number, peer in enumerate(peers(axis)):
            copy = pltpu.make_async_remote_copy(
                source, slots.at[number], send.at[number], recv.at[number], device_id=peer, device_id_type=MESH
            )
            copy.start()
            here.append(copy)
        for copy in here:
            copy.wait_recv()
        copies += here
        merged = merge([source[...]] + [slots[number] for number in range(len(here))])
        if axis == "grp":
            mid[...] = merged
            source = mid
    for copy in copies:
        copy.wait_send()
    return merged


def norm_rows(merged):
    total, spread, count = merged[0:1], merged[1:2], merged[2:3]
    return jnp.concatenate([total / count, lax.rsqrt(spread / count + eps_norm), count], axis=0)


def clear_edges(col, images, reverse):
    for tap_row in range(3):
        for tap_col in range(3):
            tap = 3 * tap_row + tap_col
            dy, dx = (1 - tap_row, 1 - tap_col) if reverse else (tap_row - 1, tap_col - 1)
            for row in range(SIDE):
                for column in range(SIDE):
                    inside = 0 <= row + dy < SIDE and 0 <= column + dx < SIDE
                    if not inside:
                        at = (row * SIDE + column) * images
                        col[at : at + images, tap * BLK : (tap + 1) * BLK] = jnp.zeros((images, BLK), BF16)


def spread_row(col, value, row, images, reverse):
    for tap_row in range(3):
        for tap_col in range(3):
            tap = 3 * tap_row + tap_col
            dy, dx = (1 - tap_row, 1 - tap_col) if reverse else (tap_row - 1, tap_col - 1)
            to_row = row - dy
            if not 0 <= to_row < SIDE:
                continue
            first = max(0, dx)
            last = min(SIDE, SIDE + dx)
            at = (to_row * SIDE + first - dx) * images
            col[at : at + (last - first) * images, tap * BLK : (tap + 1) * BLK] = value[first * images : last * images]


class Links:
    def __init__(self, send, recv, local):
        self.send_sems, self.recv_sems, self.local_sems = send, recv, local
        self.sent = self.moved = 0
        self.open_sends, self.open_moves = [], []

    def send(self, source, target, peer):
        at = self.sent
        self.sent += 1
        copy = pltpu.make_async_remote_copy(
            source, target, self.send_sems.at[at], self.recv_sems.at[at], device_id=peer, device_id_type=MESH
        )
        copy.start()
        self.open_sends.append(copy)
        return copy

    def move(self, source, target, keep=True):
        copy = pltpu.make_async_copy(source, target, self.local_sems.at[self.moved])
        self.moved += 1
        copy.start()
        if keep:
            self.open_moves.append(copy)
        return copy

    def close(self):
        for copy in self.open_sends:
            copy.wait_send()
        for copy in self.open_moves:
            copy.wait()


def arrived(copies):
    for copy in copies:
        copy.wait_recv()


class Place:
    def __init__(self):
        grp, batch = lax.axis_size("grp"), lax.axis_size("batch")
        self.grp, self.lines = grp, batch // 2
        self.me, self.mine = lax.axis_index("grp"), lax.axis_index("batch")
        self.core, self.line = lax.rem(self.mine, 2), self.mine // 2
        self.sibling = {"batch": self.mine + 1 - 2 * self.core}
        self.across = peers("grp")
        self.along = [{"batch": self.next_line(k) * 2 + self.core} for k in range(1, self.lines)]
        self.far = {"batch": (self.line + 2 - 4 * (self.line // 2)) * 2 + self.core}
        self.near = {"batch": (self.line + 1 - 2 * lax.rem(self.line, 2)) * 2 + self.core}

    def next_grp(self, k):
        return lax.rem(self.me + k, self.grp)

    def next_line(self, k):
        return lax.rem(self.line + k, self.lines)


def aligned(at, size):
    return pl.ds(pl.multiple_of(at, size), size)


def block_weights(wg_ref, number, blocks):
    lanes = lax.broadcasted_iota(jnp.int32, (GW, 128), 1) // GW
    zero = jnp.zeros((GW, 128), BF16)
    for group in range(BLK // GW):
        for tap in range(9):
            piece = wg_ref[number, group // 2, group % 2, (tap // 4) * GW : (tap // 4 + 1) * GW].astype(F32)
            turn = ((group - tap) % 4) * GW
            if turn:
                piece = pltpu.roll(piece, turn, 1)
            piece = jnp.where(lanes == group % 4, piece, 0.0).astype(BF16)
            row = tap * BLK + group * GW
            left = (group // 4) * 128
            blocks[row : row + GW, left : left + 128] = piece
            blocks[row : row + GW, 128 - left : 256 - left] = zero


def block_stats(z_ref, left, columns, m_ref, st_ref, step):
    rows = z_ref.shape[0]
    for part in range(0, columns, BLK):
        span = pl.ds(pl.multiple_of(left + part, BLK), BLK)
        total = jnp.zeros((1, BLK), F32)
        count = jnp.zeros((1, 128), F32)
        for at in range(0, rows, step):
            mask = m_ref[at : at + step]
            total += jnp.sum(z_ref[at : at + step, span] * wide(mask, BLK), axis=0, keepdims=True)
            count += jnp.sum(mask, axis=0, keepdims=True)
        count = wide(count, BLK)
        centre = total / count
        spread = jnp.zeros((1, BLK), F32)
        for at in range(0, rows, step):
            off = (z_ref[at : at + step, span] - centre) * wide(m_ref[at : at + step], BLK)
            spread += jnp.sum(off * off, axis=0, keepdims=True)
        st_ref[0:1, span] = total
        st_ref[1:2, span] = spread
        st_ref[2:3, span] = count


def smooth(pre, mask):
    sigma = sigmoid(pre)
    masked = sigma * mask
    return pre * masked, masked * (1.0 + pre * (1.0 - sigma))


FWD_OUTS = ("inner", "x1", "act1", "slope1", "x2", "act2", "slope2", "x3", "grads", "outs", "wr", "we", "wg")


def forward_kernel(*refs, images, gather):
    (feat, cotg, m_ref, np_ref, op_ref, wr_in, we_in, wg_in) = refs[:8]
    big = dict(zip(FWD_OUTS, refs[8:21]))
    n1, n2, n3, norm_all, out_all, sums3 = refs[21:27]
    (inner, x1, act1, slope1, x2, act2, slope2, x3, grads, land_f, wr, we, wg) = refs[27:40]
    (land_c, cot, perm, back, z1, ze, col, blocks, st1, st2, st3, st4, send, recv, moves) = refs[40:55]
    ex1, ex2, ex3, ex4 = (refs[55 + 7 * k : 62 + 7 * k] for k in range(4))
    held = dict(zip(FWD_OUTS, (inner, x1, act1, slope1, x2, act2, slope2, x3, grads, land_f, wr, we, wg)))
    here = Place()
    grp = here.grp
    rows, own_in = land_f.shape[1:]
    width, channels = z1.shape[1], ze.shape[1]
    own_width = np_ref.shape[1]
    step = SIDE * images
    links = Links(send, recv, moves)

    greet(everyone())
    own_rows = aligned(here.me * rows, rows)
    own_f = links.move(feat.at[own_rows], land_f.at[0], keep=False)
    if gather:
        wr[here.me, here.line, here.core] = wr_in[...]
        we[here.me, here.line, here.core] = we_in[...]
        wg[here.me, here.line, here.core] = wg_in[...]
        loads = []
    else:
        loads = [links.move(wr_in, wr, keep=False), links.move(we_in, we, keep=False), links.move(wg_in, wg, keep=False)]
    norm_all[:, aligned(here.me * own_width, own_width)] = np_ref[...]
    out_all[:, aligned(here.me * own_in, own_in)] = op_ref[...]
    greeted(everyone())

    def spread_out(buffer, targets, rows=slice(None)):
        place = buffer.at[here.me, here.line, here.core, rows]
        return [links.send(place, place, peer) for peer in targets]

    if gather:
        wr_a = spread_out(wr, here.across)
        wg_a = spread_out(wg, here.across)
    small = []
    for k in range(1, grp):
        peer = here.across[k - 1]
        span = aligned(here.me * own_width, own_width)
        small.append(links.send(np_ref, norm_all.at[:, span], peer))
        span = aligned(here.me * own_in, own_in)
        small.append(links.send(op_ref, out_all.at[:, span], peer))
    from_f = {}
    for k in range(1, grp):
        source = feat.at[aligned(here.next_grp(k) * rows, rows)]
        from_f[grp - k] = links.send(source, land_f.at[grp - k], here.across[k - 1])
    own_c = links.move(cotg.at[own_rows], land_c.at[0], keep=False)
    if gather:
        arrived(wr_a)
        wr_b = [links.send(wr.at[:, here.line, here.core], wr.at[:, here.line, here.core], here.sibling)]
        wr_l = [links.send(wr.at[:, here.line, here.core], wr.at[:, here.line, here.core], peer) for peer in here.along]
        arrived(wg_a)
        wg_b = [links.send(wg.at[:, here.line, here.core], wg.at[:, here.line, here.core], peer) for peer in here.along]
    perm[...] = to_inner(rows, images)
    back[...] = to_outer(rows, images)
    own_f.wait()
    for number in range(grp):
        if number:
            from_f[number].wait_recv()
        span = aligned(here.next_grp(number) * own_in, own_in)
        inner[:, span] = dot(perm[...], land_f[number]).astype(BF16)
    if gather:
        for k in range(1, here.lines):
            wr_l[k - 1].wait_recv()
            line = here.next_line(here.lines - k)
            wr_b.append(links.send(wr.at[:, line, here.core], wr.at[:, line, here.core], here.sibling))
        arrived(wg_b)
        wg_c = [links.send(wg.at[:, :, here.core], wg.at[:, :, here.core], here.sibling)]
        arrived(wr_b)
    for copy in loads:
        copy.wait()
    links.move(inner, big["inner"])

    if gather:
        half = we.shape[3] // 2
        lower, upper = pl.ds(0, half), pl.ds(half, half)
        we_a0 = spread_out(we, here.across, lower)
        we_a1 = spread_out(we, here.along, upper)
    from_c = {}
    for k in range(1, grp):
        source = cotg.at[aligned(here.next_grp(k) * rows, rows)]
        from_c[grp - k] = links.send(source, land_c.at[grp - k], here.across[k - 1])

    steps = width // BLK

    @pl.loop(0, steps)
    def _(number):
        span = aligned(number * BLK, BLK)
        z1[:, span] = dot(inner[...], wr[:, :, :, :, span].reshape(channels, BLK))
        block_stats(z1, number * BLK, BLK, m_ref, st1, step)

    links.move(wr, big["wr"])
    if gather:
        arrived(we_a0)
        arrived(we_a1)
        we_b = [
            links.send(we.at[:, here.line, here.core, lower], we.at[:, here.line, here.core, lower], peer)
            for peer in here.along
        ] + [
            links.send(we.at[here.me, :, here.core, upper], we.at[here.me, :, here.core, upper], peer)
            for peer in here.across
        ]
        arrived(wg_c)
    arrived(small)
    n1[...] = norm_rows(over_devices(st1, ex1, merge_stats))

    clear_edges(col, images, False)

    @pl.loop(0, steps)
    def _(number):
        span = aligned(number * BLK, BLK)
        block_weights(wg, number, blocks)
        centre, scale = n1[0:1, span], n1[1:2, span]
        gain, bias = norm_all[0:1, span], norm_all[1:2, span]
        for row in range(SIDE):
            at = row * step
            mask = wide(m_ref[at : at + step], BLK)
            normed = (z1[at : at + step, span] - centre) * scale
            value, slope = smooth(normed * gain + bias, mask)
            act = value.astype(BF16)
            x1[at : at + step, span] = normed.astype(BF16)
            act1[at : at + step, span] = act
            slope1[at : at + step, span] = slope.astype(BF16)
            spread_row(col, act, row, images, False)
        z1[:, span] = dot(col[...], blocks[...])
        block_stats(z1, number * BLK, BLK, m_ref, st2, step)

    for name in ("x1", "act1", "slope1", "wg"):
        links.move(held[name], big[name])
    if gather:
        arrived(we_b)
        we_c = [links.send(we.at[:, :, here.core], we.at[:, :, here.core], here.sibling)]
    n2[...] = norm_rows(over_devices(st2, ex2, merge_stats))

    @pl.loop(0, steps)
    def _(number):
        span = aligned(number * BLK, BLK)
        for at in range(0, rows, step):
            mask = wide(m_ref[at : at + step], BLK)
            normed = (z1[at : at + step, span] - n2[0:1, span]) * n2[1:2, span]
            value, slope = smooth(normed * norm_all[2:3, span] + norm_all[3:4, span], mask)
            x2[at : at + step, span] = normed.astype(BF16)
            act2[at : at + step, span] = value.astype(BF16)
            slope2[at : at + step, span] = slope.astype(BF16)

    for name in ("x2", "act2", "slope2"):
        links.move(held[name], big[name])
    if gather:
        arrived(we_c)
    links.move(we, big["we"])

    @pl.loop(0, grp)
    def _(number):
        for part in range(0, own_in, BLK):
            span = pl.ds(pl.multiple_of(number * own_in + part, BLK), BLK)
            ze[:, span] = dot(act2[...], we[number, :, :, :, part : part + BLK].reshape(width, BLK))
        block_stats(ze, number * own_in, own_in, m_ref, st3, step)

    n3[...] = norm_rows(over_devices(st3, ex3, merge_stats))
    own_c.wait()
    arrived([from_c[number] for number in range(1, grp)])

    @pl.loop(0, grp)
    def _(number):
        slot = lax.rem(number + grp - here.me, grp)
        cot[...] = dot(perm[...], land_c[slot])
        for part in range(0, own_in, BLK):
            span = pl.ds(pl.multiple_of(number * own_in + part, BLK), BLK)
            local = slice(part, part + BLK)
            bias_grad = jnp.zeros((1, BLK), F32)
            gain_grad = jnp.zeros((1, BLK), F32)
            for at in range(0, rows, step):
                mask = wide(m_ref[at : at + step], BLK)
                normed = (ze[at : at + step, span] - n3[0:1, span]) * n3[1:2, span]
                summed = normed * out_all[0:1, span] + out_all[1:2, span] + inner[at : at + step, span].astype(F32)
                value, slope = smooth(summed, mask)
                grad = cot[at : at + step, local] * slope
                x3[at : at + step, span] = normed.astype(BF16)
                col[at : at + step, local] = value.astype(BF16)
                grads[at : at + step, span] = grad.astype(BF16)
                bias_grad += jnp.sum(grad, axis=0, keepdims=True)
                gain_grad += jnp.sum(grad * normed, axis=0, keepdims=True)
            st4[0:1, span] = bias_grad
            st4[1:2, span] = gain_grad
        land_f[slot] = dot(back[...], col[:, 0:own_in]).astype(BF16)

    for name in ("x3", "grads", "outs"):
        links.move(held[name], big[name])
    sums3[...] = over_devices(st4, ex4, add_rows)
    links.close()


def forward(features, out_cotangent, mask, norm_params, out_params, reduce_w, expand_w, group_w, gather):
    grp = lax.axis_size("grp")
    rows = features.shape[0] // grp
    own_in = features.shape[1]
    channels = own_in * grp
    width = norm_params.shape[1] * grp
    lines, cores = (lax.axis_size("batch") // 2, 2) if gather else (1, 1)
    r_shape = (grp, lines, cores, own_in // (lines * cores), width)
    e_shape = (grp, lines, cores, width // (lines * cores), own_in)
    g_shape = (width // BLK, BLK // GW // 2, 2, 3 * GW, 128)
    across = (rows, width)
    shapes = {
        "inner": (rows, channels),
        "x1": across,
        "act1": across,
        "slope1": across,
        "x2": across,
        "act2": across,
        "slope2": across,
        "x3": (rows, channels),
        "grads": (rows, channels),
        "outs": (grp, rows, own_in),
        "wr": r_shape,
        "we": e_shape,
        "wg": g_shape,
    }
    small = [(3, width), (3, width), (3, channels), (4, width), (2, channels), (2, channels)]
    vmem = pl.BlockSpec(memory_space=pltpu.VMEM)
    hbm = pl.BlockSpec(memory_space=pl.ANY)
    if gather:
        weights = (reduce_w, expand_w, group_w)
    else:
        weights = (reduce_w.reshape(r_shape), expand_w.reshape(e_shape), group_w.reshape(g_shape))
    results = pl.pallas_call(
        functools.partial(forward_kernel, images=rows // HW, gather=gather),
        out_shape=[jax.ShapeDtypeStruct(shapes[name], BF16) for name in FWD_OUTS]
        + [jax.ShapeDtypeStruct(shape, F32) for shape in small],
        in_specs=[hbm, hbm, vmem, vmem, vmem] + [vmem if gather else hbm] * 3,
        out_specs=[hbm] * len(FWD_OUTS) + [vmem] * len(small),
        scratch_shapes=[pltpu.VMEM(shapes[name], BF16) for name in FWD_OUTS]
        + [
            pltpu.VMEM((grp, rows, own_in), BF16),
            pltpu.VMEM((rows, own_in), F32),
            pltpu.VMEM((rows, rows), BF16),
            pltpu.VMEM((rows, rows), BF16),
            pltpu.VMEM(across, F32),
            pltpu.VMEM((rows, channels), F32),
            pltpu.VMEM((rows, 9 * BLK), BF16),
            pltpu.VMEM((9 * BLK, BLK), BF16),
            pltpu.VMEM((3, width), F32),
            pltpu.VMEM((3, width), F32),
            pltpu.VMEM((3, channels), F32),
            pltpu.VMEM((2, channels), F32),
            pltpu.SemaphoreType.DMA((64,)),
            pltpu.SemaphoreType.DMA((64,)),
            pltpu.SemaphoreType.DMA((20,)),
        ]
        + sums_scratch(3, width)
        + sums_scratch(3, width)
        + sums_scratch(3, channels)
        + sums_scratch(2, channels),
        compiler_params=params(collective_id=1, has_side_effects=True),
    )(features, out_cotangent, mask, norm_params, out_params, *weights)
    return dict(zip(FWD_OUTS, results)), results[len(FWD_OUTS) :]


def packed_groups(weight):
    groups = weight.shape[1] // GW
    taps = jnp.pad(weight.reshape(9, GW, groups, GW), ((0, 3), (0, 0), (0, 0), (0, 0)))
    return taps.reshape(3, 4, GW, groups, GW).transpose(3, 0, 2, 1, 4).reshape(groups, 3 * GW, 4 * GW)


BWD_INS = ("grads", "x3", "we", "act2", "slope2", "x2", "act1", "slope1", "x1", "wg", "wr")


def backward_kernel(*refs, images, owners):
    outs_in, inner_in = refs[:2]
    given = dict(zip(BWD_INS, refs[2:13]))
    m_ref, n1, n2, n3, norm_all, out_all, sums3 = refs[13:20]
    block_out, input_grad, reduce_out, expand_out, group_out, sums1, sums2 = refs[20:27]
    (grads, x3, we, act2, slope2, x2, act1, slope1, x1, wg, wr) = refs[27:38]
    held = dict(zip(BWD_INS, (grads, x3, we, act2, slope2, x2, act1, slope1, x1, wg, wr)))
    (ge, dp, col, blocks, turned, grad_in, back, st1, st2, raw_e, raw_r, raw_g, send, recv, moves) = refs[38:53]
    ex1, ex2 = refs[53:60], refs[60:67]
    here = Place()
    me, grp, core, line, lines = here.me, here.grp, here.core, here.line, here.lines
    rows, width = dp.shape
    channels = grads.shape[1]
    own_in = channels // grp
    step = SIDE * images
    steps = width // BLK
    links = Links(send, recv, moves)
    if owners:
        (e1, e2, e3, r1, r2, r3, g1, g2, g3, g4, gs1, gs2, gs3) = refs[67:]

    greet(everyone())
    loads = {name: links.move(given[name], held[name], keep=False) for name in BWD_INS}
    own_rows = aligned(me * rows, rows)
    links.move(outs_in.at[0], block_out.at[own_rows])
    back[...] = to_outer(rows, images)
    greeted(everyone())
    out_sends = [
        links.send(outs_in.at[k], block_out.at[own_rows], here.across[k - 1]) for k in range(1, grp)
    ]

    def core_swap(raw, slot):
        return links.send(raw.at[:, :, 1 - core], slot, here.sibling)

    def add_core(raw, slot):
        @pl.loop(0, grp * lines)
        def _(at):
            a, b = at // lines, lax.rem(at, lines)
            slot[a, b] = (raw[a, b, core].astype(F32) + slot[a, b].astype(F32)).astype(BF16)

    def over_grp(summed, slots):
        return [links.send(summed.at[here.next_grp(k)], slots.at[k - 1], here.across[k - 1]) for k in range(1, grp)]

    def add_grp(summed, slots):
        @pl.loop(0, lines)
        def _(b):
            piece = summed[me, b].astype(F32)
            for k in range(grp - 1):
                piece += slots[k, b].astype(F32)
            slots[0, b] = piece.astype(BF16)

    def over_line(slots, last):
        return [
            links.send(slots.at[0, here.next_line(k)], last.at[k - 1], here.along[k - 1]) for k in range(1, lines)
        ]

    def add_line(slots, last, out):
        piece = slots[0, line].astype(F32)
        for k in range(lines - 1):
            piece += last[k].astype(F32)
        out[...] = piece

    for name in ("grads", "x3", "we", "act2"):
        loads[name].wait()

    @pl.loop(0, grp)
    def _(number):
        for part in range(0, own_in, BLK):
            span = pl.ds(pl.multiple_of(number * own_in + part, BLK), BLK)
            inverse = 1.0 / n3[2:3, span]
            factor = out_all[0:1, span] * n3[1:2, span]
            for at in range(0, rows, step):
                mask = wide(m_ref[at : at + step], BLK)
                normed = x3[at : at + step, span].astype(F32)
                shift = (sums3[0:1, span] + normed * sums3[1:2, span]) * inverse
                value = mask * factor * (grads[at : at + step, span].astype(F32) - shift)
                ge[at : at + step, part : part + BLK] = value.astype(BF16)
        per = we.shape[3]
        taken = BLK // per if per < BLK else 1
        for left in range(0, width, BLK):
            if per < BLK:
                slots = [divmod(left // per + k, we.shape[2]) for k in range(taken)]
                weights = jnp.concatenate([we[number, b, c] for b, c in slots], axis=0)
            else:
                weights = we[number, 0, 0, left : left + BLK]
            part_sum = dot_right(ge[...], weights)
            block = dot_left(act2[:, left : left + BLK], ge[...]).astype(BF16)
            if per < BLK:
                for k, (b, c) in enumerate(slots):
                    raw_e[number, b, c] = block[k * per : (k + 1) * per]
            else:
                raw_e[number, 0, 0, left : left + BLK] = block

            @pl.when(number == 0)
            def _():
                dp[:, left : left + BLK] = part_sum

            @pl.when(number > 0)
            def _():
                dp[:, left : left + BLK] += part_sum

    if owners:
        e_core = core_swap(raw_e, e1)
    else:
        links.move(raw_e, expand_out)
    for name in ("slope2", "x2"):
        loads[name].wait()

    def norm_sums(slope, normed, sums):
        @pl.loop(0, steps)
        def _(number):
            span = aligned(number * BLK, BLK)
            bias_grad = jnp.zeros((1, BLK), F32)
            gain_grad = jnp.zeros((1, BLK), F32)
            for at in range(0, rows, step):
                grad = dp[at : at + step, span] * slope[at : at + step, span].astype(F32)
                dp[at : at + step, span] = grad
                bias_grad += jnp.sum(grad, axis=0, keepdims=True)
                gain_grad += jnp.sum(grad * normed[at : at + step, span].astype(F32), axis=0, keepdims=True)
            sums[0:1, span] = bias_grad
            sums[1:2, span] = gain_grad

    norm_sums(slope2, x2, st2)
    sums2[...] = over_devices(st2, ex2, add_rows)
    if owners:
        e_core.wait_recv()
        add_core(raw_e, e1)
        e_grp = over_grp(e1, e2)

    for name in ("act1", "slope1", "x1", "wg"):
        loads[name].wait()
    own = (
        lax.broadcasted_iota(jnp.int32, (BLK, BLK), 0) // GW == lax.broadcasted_iota(jnp.int32, (BLK, BLK), 1) // GW
    )

    @pl.loop(0, steps)
    def _(number):
        span = aligned(number * BLK, BLK)
        inverse = 1.0 / n2[2:3, span]
        factor = norm_all[2:3, span] * n2[1:2, span]
        clear_edges(col, images, False)
        for row in range(SIDE):
            at = row * step
            mask = wide(m_ref[at : at + step], BLK)
            normed = x2[at : at + step, span].astype(F32)
            shift = (sums2[0:1, span] + normed * sums2[1:2, span]) * inverse
            grad_in[at : at + step] = (mask * factor * (dp[at : at + step, span] - shift)).astype(BF16)
            spread_row(col, act1[at : at + step, span], row, images, False)
        for tap in range(9):
            product = dot_left(col[:, tap * BLK : (tap + 1) * BLK], grad_in[...])
            product = jnp.where(own, product, 0.0)
            piece = product[0:GW]
            for group in range(1, BLK // GW):
                piece += product[group * GW : (group + 1) * GW]
            raw_g[tap * GW : (tap + 1) * GW, span] = piece.astype(BF16)
        clear_edges(col, images, True)
        for row in range(SIDE):
            at = row * step
            spread_row(col, grad_in[at : at + step], row, images, True)
        block_weights(wg, number, blocks)
        for tap in range(9):
            turned[tap * BLK : (tap + 1) * BLK] = blocks[tap * BLK : (tap + 1) * BLK].astype(F32).T.astype(BF16)
        dp[:, span] = dot(col[...], turned[...])

    norm_sums(slope1, x1, st1)
    inner = col.at[:, 0:channels]
    load_inner = links.move(inner_in, inner, keep=False)
    if owners:
        g_grp = [
            links.send(raw_g.at[:, aligned(here.next_grp(k) * BLK, BLK)], g1.at[k - 1], here.across[k - 1])
            for k in range(1, grp)
        ]
    else:
        links.move(raw_g, group_out)
    sums1[...] = over_devices(st1, ex1, add_rows)
    if owners:
        arrived(e_grp)
        add_grp(e1, e2)
        e_line = over_line(e2, e3)

    @pl.loop(0, steps)
    def _(number):
        span = aligned(number * BLK, BLK)
        inverse = 1.0 / n1[2:3, span]
        factor = norm_all[0:1, span] * n1[1:2, span]
        for at in range(0, rows, step):
            mask = wide(m_ref[at : at + step], BLK)
            normed = x1[at : at + step, span].astype(F32)
            shift = (sums1[0:1, span] + normed * sums1[1:2, span]) * inverse
            x1[at : at + step, span] = (mask * factor * (dp[at : at + step, span] - shift)).astype(BF16)

    grad_reduce = x1
    load_inner.wait()
    per_r = raw_r.shape[3]

    @pl.loop(0, grp)
    def _(number):
        for part in range(0, own_in, BLK):
            span = pl.ds(pl.multiple_of(number * own_in + part, BLK), BLK)
            block = dot_left(col[:, span], grad_reduce[...]).astype(BF16)
            if per_r < BLK:
                for k in range(BLK // per_r):
                    b, c = divmod(part // per_r + k, raw_r.shape[2])
                    raw_r[number, b, c] = block[k * per_r : (k + 1) * per_r]
            else:
                raw_r[number, 0, 0, part : part + BLK] = block

    if owners:
        r_core = core_swap(raw_r, r1)
        arrived(g_grp)
        total = raw_g[:, aligned(me * BLK, BLK)].astype(F32)
        for k in range(grp - 1):
            total += g1[k].astype(F32)
        gs1[...] = total.astype(BF16)
        high = line // 2
        g_far = links.send(gs1.at[:, aligned((1 - high) * 128, 128)], g2, here.far)
        r_core.wait_recv()
        add_core(raw_r, r1)
        r_grp = over_grp(r1, r2)
    else:
        links.move(raw_r, reduce_out)
    loads["wr"].wait()

    @pl.loop(0, grp)
    def _(number):
        for part in range(0, own_in, BLK):
            span = pl.ds(pl.multiple_of(number * own_in + part, BLK), BLK)
            per = wr.shape[3]
            if per < BLK:
                slots = [divmod(part // per + k, wr.shape[2]) for k in range(BLK // per)]
                weights = jnp.concatenate([wr[number, b, c] for b, c in slots], axis=0)
            else:
                weights = wr[number, 0, 0, part : part + BLK]
            total = grads[:, span].astype(F32) + dot_right(grad_reduce[...], weights)
            ge[:, part : part + BLK] = total.astype(BF16)
        grads[:, aligned(number * own_in, own_in)] = dot(back[...], ge[...]).astype(BF16)

    if owners:
        g_far.wait_recv()
        gs2[...] = (gs1[:, aligned(high * 128, 128)].astype(F32) + g2[...].astype(F32)).astype(BF16)
        g_near = links.send(gs2, g3, here.near)
        arrived(e_line)
        add_line(e2, e3, expand_out)
        g_near.wait_recv()
        gs3[...] = (gs2[...].astype(F32) + g3[...].astype(F32)).astype(BF16)
        g_last = links.send(gs3, g4, here.sibling)
        g_last.wait_recv()
        group_out[...] = gs3[...].astype(F32) + g4[...].astype(F32)
        arrived(r_grp)
        add_grp(r1, r2)
        r_line = over_line(r2, r3)
    in_sends = [
        links.send(grads.at[:, aligned(here.next_grp(k) * own_in, own_in)], input_grad.at[own_rows], here.across[k - 1])
        for k in range(1, grp)
    ]
    links.move(grads.at[:, aligned(me * own_in, own_in)], input_grad.at[own_rows])
    if owners:
        arrived(r_line)
        add_line(r2, r3, reduce_out)
    arrived(out_sends)
    arrived(in_sends)
    links.close()


def backward(kept, mask, n1, n2, n3, norm_all, out_all, sums3, owners):
    grp = lax.axis_size("grp")
    rows, width = kept["act1"].shape
    channels = kept["x3"].shape[1]
    own_in = channels // grp
    r_shape, e_shape = kept["wr"].shape, kept["we"].shape
    lines = r_shape[1]
    vmem = pl.BlockSpec(memory_space=pltpu.VMEM)
    hbm = pl.BlockSpec(memory_space=pl.ANY)
    if owners:
        parts = [
            jax.ShapeDtypeStruct(r_shape[3:], F32),
            jax.ShapeDtypeStruct(e_shape[3:], F32),
            jax.ShapeDtypeStruct((9 * GW, 128), F32),
        ]
    else:
        parts = [jax.ShapeDtypeStruct(shape, BF16) for shape in (r_shape, e_shape, (9 * GW, width))]
    sums = [jax.ShapeDtypeStruct((2, width), F32)] * 2
    scratch = [pltpu.VMEM(kept[name].shape, BF16) for name in BWD_INS] + [
        pltpu.VMEM((rows, own_in), BF16),
        pltpu.VMEM((rows, width), F32),
        pltpu.VMEM((rows, 9 * BLK), BF16),
        pltpu.VMEM((9 * BLK, BLK), BF16),
        pltpu.VMEM((9 * BLK, BLK), BF16),
        pltpu.VMEM((rows, BLK), BF16),
        pltpu.VMEM((rows, rows), BF16),
        pltpu.VMEM((2, width), F32),
        pltpu.VMEM((2, width), F32),
        pltpu.VMEM(e_shape, BF16),
        pltpu.VMEM(r_shape, BF16),
        pltpu.VMEM((9 * GW, width), BF16),
        pltpu.SemaphoreType.DMA((32,)),
        pltpu.SemaphoreType.DMA((32,)),
        pltpu.SemaphoreType.DMA((20,)),
    ]
    scratch += sums_scratch(2, width) + sums_scratch(2, width)
    if owners:
        for shape in (e_shape, r_shape):
            tail = shape[3:]
            scratch += [
                pltpu.VMEM((grp, lines, *tail), BF16),
                pltpu.VMEM((grp - 1, lines, *tail), BF16),
                pltpu.VMEM((lines - 1, *tail), BF16),
            ]
        narrow = pltpu.VMEM((9 * GW, 128), BF16)
        scratch += [pltpu.VMEM((grp - 1, 9 * GW, BLK), BF16), narrow, narrow, narrow]
        scratch += [pltpu.VMEM((9 * GW, BLK), BF16), narrow, narrow]
    whole = jax.ShapeDtypeStruct((grp * rows, own_in), BF16)
    return pl.pallas_call(
        functools.partial(backward_kernel, images=rows // HW, owners=owners),
        out_shape=[whole, whole, *parts, *sums],
        in_specs=[hbm] * 13 + [vmem] * 7,
        out_specs=[hbm, hbm] + [vmem if owners else hbm] * 3 + [vmem] * 2,
        scratch_shapes=scratch,
        compiler_params=params(collective_id=2, has_side_effects=True),
    )(
        kept["outs"],
        kept["inner"],
        *[kept[name] for name in BWD_INS],
        mask,
        n1,
        n2,
        n3,
        norm_all,
        out_all,
        sums3,
    )


DECAYS = (0.01, 0.01, 0.01, 0.0, 0.0)


def whole_sum(value):
    return jnp.sum(jnp.sum(value, axis=0, keepdims=True), axis=1, keepdims=True)


def adam_direction(tensor, clipped, moment_one, moment_two, decay_rate):
    new_first = beta_one * moment_one + (1.0 - beta_one) * clipped
    new_second = beta_two * moment_two + (1.0 - beta_two) * clipped * clipped
    first_hat = new_first / (1.0 - beta_one**step_count)
    second_hat = new_second / (1.0 - beta_two**step_count)
    direction = first_hat / (jnp.sqrt(second_hat) + adam_eps) + decay_rate * tensor
    return (new_first, new_second, direction)


def trust_kernel(*refs):
    raws, tensors, firsts, seconds = (refs[5 * k : 5 * k + 5] for k in range(4))
    out_ref, pay, *scratch = refs[20:]
    one, two = scratch[:7], scratch[7:]
    share = 1.0 / lax.axis_size("batch")
    shares = (1.0, 1.0, 1.0, share, share)
    greet(everyone())
    square = jnp.zeros((1, 1), F32)
    pay[...] = jnp.zeros_like(pay)
    for number in range(5):
        square += shares[number] * whole_sum(raws[number][...] ** 2)
        weight = shares[number] * whole_sum(tensors[number][...] ** 2)
        pay[0, number + 1 : number + 2] = jnp.broadcast_to(weight, (1, 128))
    pay[0, 0:1] = jnp.broadcast_to(square, (1, 128))
    greeted(everyone())
    sums = over_devices(pay.at[0], one, add_rows)
    grad_norm = jnp.sqrt(sums[0:1])
    factor = jnp.minimum(1.0, clip_norm / grad_norm)
    for number in range(5):
        direction = adam_direction(
            tensors[number][...],
            factor[0:1, 0:1] * raws[number][...],
            firsts[number][...],
            seconds[number][...],
            DECAYS[number],
        )[2]
        step = shares[number] * whole_sum(direction * direction)
        pay[1, number + 1 : number + 2] = jnp.broadcast_to(step, (1, 128))
    steps = over_devices(pay.at[1], two, add_rows)
    out_ref[...] = jnp.zeros_like(out_ref)
    out_ref[0:1] = grad_norm
    out_ref[1:2] = factor
    out_ref[2:7] = jnp.sqrt(sums[1:6]) * lax.rsqrt(steps[1:6] + 1e-06)


def update_kernel(*refs):
    scalars = refs[0]
    raws, tensors, firsts, seconds = (refs[5 * k + 1 : 5 * k + 6] for k in range(4))
    outs = refs[21:]
    at = 0
    for number in range(5):
        clipped = scalars[1:2, 0:1] * raws[number][...]
        tensor = tensors[number][...]
        new_first, new_second, direction = adam_direction(
            tensor, clipped, firsts[number][...], seconds[number][...], DECAYS[number]
        )
        updated = tensor - learn_rate * scalars[2 + number : 3 + number, 0:1] * direction
        values = [clipped, new_first, new_second, updated]
        if number < 3:
            values.append(updated.astype(BF16))
        for value in values:
            outs[at][...] = value
            at += 1


def optimizer(raws, tensors, firsts, seconds):
    vmem = pl.BlockSpec(memory_space=pltpu.VMEM)
    state = (*raws, *tensors, *firsts, *seconds)
    scalars = pl.pallas_call(
        trust_kernel,
        out_shape=jax.ShapeDtypeStruct((8, 128), F32),
        in_specs=[vmem] * 20,
        out_specs=vmem,
        scratch_shapes=[pltpu.VMEM((2, 8, 128), F32)] + sums_scratch(8, 128) + sums_scratch(8, 128),
        compiler_params=params(collective_id=8, has_side_effects=True),
    )(*state)
    shapes = []
    for number, tensor in enumerate(tensors):
        shapes += [jax.ShapeDtypeStruct(tensor.shape, F32)] * 4
        if number < 3:
            shapes.append(jax.ShapeDtypeStruct(tensor.shape, BF16))
    outs = pl.pallas_call(
        update_kernel,
        out_shape=shapes,
        in_specs=[vmem] * 21,
        out_specs=[vmem] * len(shapes),
        compiler_params=params(),
    )(scalars, *state)
    return scalars, outs


def local(
    features,
    pixel_mask,
    out_cotangent,
    reduce_master,
    group_master,
    expand_master,
    norm_params,
    out_params,
    reduce_first,
    reduce_second,
    group_first,
    group_second,
    expand_first,
    expand_second,
    norm_first,
    norm_second,
    out_first,
    out_second,
):
    grp, batch = lax.axis_size("grp"), lax.axis_size("batch")
    both = ("grp", "batch")
    me, mine = lax.axis_index("grp"), lax.axis_index("batch")
    rows = features.shape[0] // grp
    images = rows // HW
    own_in = features.shape[1]
    own_width = norm_params.shape[1]
    inside = batch == 8 and own_width == 8 * GW
    validity = lax.dynamic_slice_in_dim(pixel_mask, me * rows, rows, 0).astype(F32)
    mask = jnp.broadcast_to(validity.reshape(images, HW).T.reshape(rows, 1), (rows, 128))
    reduce_w, group_w, expand_w = (value.astype(BF16) for value in (reduce_master, group_master, expand_master))
    if inside:
        group_w = packed_groups(group_w)[0]
    else:
        reduce_w = lax.all_gather(reduce_w, both, axis=0, tiled=True)
        expand_w = lax.all_gather(expand_w, both, axis=0, tiled=True)
        group_w = packed_groups(lax.all_gather(group_w, both, axis=1, tiled=True))
    kept, (n1, n2, n3, norm_all, out_all, sums_three) = forward(
        features, out_cotangent, mask, norm_params, out_params, reduce_w, expand_w, group_w, inside
    )
    block_out, input_grad, reduce_part, expand_part, group_part, sums_one, sums_two = backward(
        kept, mask, n1, n2, n3, norm_all, out_all, sums_three, inside
    )
    if inside:
        group_part = lax.dynamic_slice_in_dim(group_part, lax.rem(mine, 4) * GW, GW, 1)
    else:
        flat = group_part.reshape(9 * GW, grp * batch, -1).transpose(1, 0, 2)
        reduce_part, expand_part, group_part = (
            lax.psum_scatter(value, both, scatter_dimension=0).astype(F32)
            for value in (
                reduce_part.reshape(grp * batch, own_in // batch, -1),
                expand_part.reshape(grp * batch, -1, own_in),
                flat,
            )
        )
    norm_sums = jnp.concatenate([sums_one[1:2], sums_one[0:1], sums_two[1:2], sums_two[0:1]], axis=0)
    norm_raw = lax.dynamic_slice_in_dim(norm_sums, me * own_width, own_width, 1)
    out_raw = lax.dynamic_slice_in_dim(
        jnp.concatenate([sums_three[1:2], sums_three[0:1]], axis=0), me * own_in, own_in, 1
    )
    scalars, updates = optimizer(
        (reduce_part, group_part, expand_part, norm_raw, out_raw),
        (reduce_master, group_master, expand_master, norm_params, out_params),
        (reduce_first, group_first, expand_first, norm_first, out_first),
        (reduce_second, group_second, expand_second, norm_second, out_second),
    )
    return (block_out, input_grad, scalars[0, 0], scalars[2:5, 0], scalars[5:7, 0], *updates)


def solution(mesh):
    in_specs = (
        P("batch", "grp"),
        P("batch"),
        P("batch", "grp"),
        P(("grp", "batch"), None),
        P(None, ("grp", "batch")),
        P("batch", "grp"),
        P(None, "grp"),
        P(None, "grp"),
        P(("grp", "batch"), None),
        P(("grp", "batch"), None),
        P(None, ("grp", "batch")),
        P(None, ("grp", "batch")),
        P("batch", "grp"),
        P("batch", "grp"),
        P(None, "grp"),
        P(None, "grp"),
        P(None, "grp"),
        P(None, "grp"),
    )
    out_specs = (
        P("batch", "grp"),
        P("batch", "grp"),
        P(),
        P(),
        P(),
        P(("grp", "batch"), None),
        P(("grp", "batch"), None),
        P(("grp", "batch"), None),
        P(("grp", "batch"), None),
        P(("grp", "batch"), None),
        P(None, ("grp", "batch")),
        P(None, ("grp", "batch")),
        P(None, ("grp", "batch")),
        P(None, ("grp", "batch")),
        P(None, ("grp", "batch")),
        P("batch", "grp"),
        P("batch", "grp"),
        P("batch", "grp"),
        P("batch", "grp"),
        P("batch", "grp"),
        P(None, "grp"),
        P(None, "grp"),
        P(None, "grp"),
        P(None, "grp"),
        P(None, "grp"),
        P(None, "grp"),
        P(None, "grp"),
        P(None, "grp"),
    )
    return jax.shard_map(local, mesh=mesh, in_specs=in_specs, out_specs=out_specs, check_vma=False)
```

time: 816 us -> 384 us (0.47)
  Pallas kernels: 0 us -> 356 us
  waiting for transfers between devices: 247 us -> 0 us
  blocking collectives: 230 us -> 0 us
  local copies, waits for them, and re-layouts: 137 us -> 21.5 us
  other arithmetic: 80.6 us -> 5.38 us
  matrix products: 73.4 us -> 0 us
  between operations: 26.1 us -> 0.82 us
  starting transfers between devices: 13.9 us -> 0 us
    pallas_call x0 -> x4, Pallas kernels: none -> 356 us  [the longest x1 177 us: forward(): pl.pallas_call(functools.partial(forward_kernel, images=rows // HW, gathe...]
    psum x11 -> x0, blocking collectives: 216 us -> none  [the longest x3 48.2 us: norm_stats(): totals, counted = lax.psum((jnp.sum(weighted, axis=0), count_here), 'batch')]
    all_gather x4 -> x0, waiting for transfers between devices: 113 us -> none  [the longest x1 67.8 us: local(): act_full = lax.all_gather(act_two, 'grp', axis=1, tiled=True)]
    reduce_scatter x2 -> x0, waiting for transfers between devices: 112 us -> none  [the longest x1 58.8 us: local(): lax.psum_scatter(matmul_right(grad_expand, expand_w).astype(jnp.bfloat16)...]
    dot_general x9 -> x0, matrix products: 73.4 us -> none  [the longest x3 27.5 us: matmul_left(): lax.dot_general(first_op, second_op, (((0,), (0,)), ((), ())), preferred_...]
    concatenate x18 -> x0, local copies, waits for them, and re-layouts: 56.2 us -> none  [frame_taps(): jnp.concatenate(pieces, axis=-1).reshape(images * SIDE * SIDE, 9 * channels)]
    reduce_sum x20 -> x0, other arithmetic: 40.1 us -> none  [the longest x2 17.7 us: norm_back(): jnp.sum(grad_out, axis=0)]
    all_to_all x3 -> x0, waiting for transfers between devices: 22.4 us -> none  [summed_on_arrival(): lax.all_to_all(split_up(value, dim, devices), axis, 0, 0, tiled=True)]
  transfers between devices with their start and end apart: 9 -> 0, of which waited for: 6 -> 0; matrix products, arithmetic and copies ran while one was open for 16% -> 0% of each run, Pallas kernels for 0% -> 0%
where the time goes in v1:
time: 384 us; the launch traced here: 383 us
  Pallas kernels  356 us (93%)
  local copies, waits for them, and re-layouts  21.5 us (6%)
  other arithmetic  5.38 us (1%)
    pallas_call x1, Pallas kernels, forward(): pl.pallas_call(functools.partial(forward_kernel, images=rows // HW, gathe...  177 us
    pallas_call x1, Pallas kernels, backward(): pl.pallas_call(functools.partial(backward_kernel, images=rows // HW, owne...  156 us
    pallas_call x1, Pallas kernels, optimizer(): pl.pallas_call(trust_kernel, out_shape=jax.ShapeDtypeStruct((8, 128), F32...  18.7 us
    unnamed x24, local copies, waits for them, and re-layouts  15.3 us

profile of v1, /device:TPU:0, one launch (start us, length us, event | category | flops | bytes accessed | tf_op | source)
XLA Modules:
  0.0 383.4 jit_solution(4702426518288846314)
XLA Ops:
  0.7 0.8 dynamic-slice_convert_fusion
  1.5 0.1 reshape.67
  1.5 0.1 copy.70
  1.6 0.1 broadcast_in_dim.7
  1.7 0.9 broadcast_in_dim.8.refs_2_.refs_13_
  2.6 0.9 copy.71.refs_6_.refs_7_
  3.5 0.0 copy-start.2
  3.6 0.1 copy.72
  3.7 0.7 squeeze_reshape.3.refs_7_
  4.4 1.6 convert_element_type.15.refs_5_
  6.0 1.6 convert_element_type.16.refs_6_
  7.6 177.3 %shard_map.393 = (bf16[784,2048]{1,0:T(8,128)(2,1)}, bf16[784,1024]{1,0:T(8,128)(2,1)}, bf16[784,1024]{1,0:T(8,128)(2,1)}, bf16[784,1024]{1,0:T(8,128)(2,1)}, bf...) custom-call(bf16[3136,512]{1,0:T(8,128)(2,1)} %refs_0_.1, ...), custom_call_target="tpu_custom_call" | custom-call | tf_op jit(solution)/shard_map/pallas_call | solution.py:499
  184.9 0.0 copy-done.2
  184.9 0.0 copy-start.3
  184.9 0.0 copy-start.4
  184.9 0.0 copy-start.5
  184.9 155.7 %shard_map.394 = (bf16[3136,512]{1,0:T(8,128)(2,1)}, bf16[3136,512]{1,0:T(8,128)(2,1)}, f32[64,1024]{1,0:T(8,128)}, f32[128,512]{1,0:T(8,128)}, f32[288,128]{1,0...) custom-call(bf16[4,784,512]{2,1,0:T(8,128)(2,1)} %get-tuple-element.77.refs_0_, ...), custom_call_target="tpu_custom_call" | custom-call | tf_op jit(solution)/shard_map/pallas_call | solution.py:852
  340.6 0.8 fusion.5
  341.4 0.7 fusion.3.refs_3_.refs_4_
  342.1 1.7 constant_dynamic-slice_fusion.refs_1_.refs_2_
  343.7 0.0 copy-done.3
  343.8 0.7 fusion.refs_4_.refs_5_
  344.4 0.0 copy-done.4
  344.4 0.8 copy.74.refs_11_.refs_12_
  345.2 0.0 copy-done.5
  345.2 0.8 copy.75.refs_16_.refs_17_
  346.0 0.0 copy-start.1
  346.0 18.7 %shard_map.395.refs_0_ = f32[8,128]{1,0:T(8,128)} custom-call(f32[64,1024]{1,0:T(8,128)} %get-tuple-element.98.refs_0_.refs_1_, f32[288,32]{1,0:T(8,128)} %constant_dynamic-slice_fusion.refs_1_.refs_2_, f32[128,512]{1,0:T(8,128)} %get-tuple-element.100.refs_2_.refs_3_, f32[4,256]{1,0:T(4,128)} %fusion.3.refs_3_.refs_4_, f32[2,512]{1,0:T(2,128)} %fusion.refs_4_.refs_5_, ...), custom_call_target="tpu_custom_call" | custom-call | tf_op jit(solution)/shard_map/pallas_call | solution.py:947
  364.7 0.0 copy-start.6
  364.7 4.0 %shard_map.396 = (f32[64,1024]{1,0:T(8,128)}, f32[64,1024]{1,0:T(8,128)}, f32[64,1024]{1,0:T(8,128)}, f32[64,1024]{1,0:T(8,128)}, bf16[64,1024]{1,0:T(8,128)(2,1...) custom-call(f32[8,128]{1,0:T(8,128)} %shard_map.395.refs_0_, ...), custom_call_target="tpu_custom_call" | custom-call | tf_op jit(solution)/shard_map/pallas_call | solution.py:960
  368.7 1.6 copy.79
  370.4 1.6 copy.80
  372.0 1.6 copy.81
  373.6 1.6 copy.82
  375.3 1.6 copy.83
  376.9 0.0 copy-done.6
  376.9 0.5 slice.33
  377.4 0.6 slice_reduce_fusion
  378.0 0.6 slice_reduce_fusion.1
  378.6 0.0 copy-done.1
  378.6 0.0 copy-start
  378.6 1.7 copy.86
  380.3 1.4 copy-done
  381.7 1.7 copy.87
  (3 shorter events, 0.0 us)
Async XLA Ops:
  3.5 181.3 %copy-start.2 = (f32[288,32]{1,0:T(8,128)}, f32[288,32]{1,0:T(8,128)S(1)}, u32[]{:S(2)}) copy-start(f32[288,32]{1,0:T(8,128)S(1)} %copy.71.refs_6_.refs_7_) | copy-start | bytes 110596
  184.9 158.9 %copy-start.3 = (f32[2,2048]{1,0:T(2,128)S(1)}, f32[2,2048]{1,0:T(2,128)}, u32[]{:S(2)}) copy-start(f32[2,2048]{1,0:T(2,128)} %get-tuple-element.95.refs_19_) | copy-start | bytes 49156
  184.9 159.5 %copy-start.4 = (f32[288,32]{0,1:T(8,128)S(1)}, f32[288,32]{0,1:T(8,128)}, u32[]{:S(2)}) copy-start(f32[288,32]{0,1:T(8,128)} %param.28) | copy-start | bytes 110596
  184.9 160.3 %copy-start.5 = (f32[288,32]{0,1:T(8,128)S(1)}, f32[288,32]{0,1:T(8,128)}, u32[]{:S(2)}) copy-start(f32[288,32]{0,1:T(8,128)} %param.29) | copy-start | bytes 110596
  346.0 32.6 %copy-start.1 = (bf16[3136,512]{1,0:T(8,128)(2,1)S(1)}, bf16[3136,512]{1,0:T(8,128)(2,1)}, u32[]{:S(2)}) copy-start(bf16[3136,512]{1,0:T(8,128)(2,1)} %get-tuple-element.246) | copy-start | bytes 9633796
  364.7 12.2 %copy-start.6 = (f32[8,128]{1,0:T(8,128)S(1)}, f32[8,128]{1,0:T(8,128)}, u32[]{:S(2)}) copy-start(f32[8,128]{1,0:T(8,128)} %shard_map.395.refs_0_) | copy-start | bytes 12292
  378.6 3.1 copy-start

commit v2 on v1

--- a/solution.py
+++ b/solution.py
@@ -170,13 +170,14 @@
         self.sent = self.moved = 0
         self.open_sends, self.open_moves = [], []
 
-    def send(self, source, target, peer):
+    def send(self, source, target, peer, start=True):
         at = self.sent
         self.sent += 1
         copy = pltpu.make_async_remote_copy(
             source, target, self.send_sems.at[at], self.recv_sems.at[at], device_id=peer, device_id_type=MESH
         )
-        copy.start()
+        if start:
+            copy.start()
         self.open_sends.append(copy)
         return copy
 
@@ -207,13 +208,14 @@
         self.me, self.mine = lax.axis_index("grp"), lax.axis_index("batch")
         self.core, self.line = lax.rem(self.mine, 2), self.mine // 2
         self.sibling = {"batch": self.mine + 1 - 2 * self.core}
-        self.across = peers("grp")
+        self.across = [{"grp": self.partner(k)} for k in range(1, grp)]
         self.along = [{"batch": self.next_line(k) * 2 + self.core} for k in range(1, self.lines)]
         self.far = {"batch": (self.line + 2 - 4 * (self.line // 2)) * 2 + self.core}
         self.near = {"batch": (self.line + 1 - 2 * lax.rem(self.line, 2)) * 2 + self.core}
 
-    def next_grp(self, k):
-        return lax.rem(self.me + k, self.grp)
+    def partner(self, k):
+        low = lax.rem(lax.rem(self.me, 2) + (k % 2 if isinstance(k, int) else lax.rem(k, 2)), 2)
+        return lax.rem(self.me // 2 + k // 2, 2) * 2 + low
 
     def next_line(self, k):
         return lax.rem(self.line + k, self.lines)
@@ -266,17 +268,17 @@
     return pre * masked, masked * (1.0 + pre * (1.0 - sigma))
 
 
-FWD_OUTS = ("inner", "x1", "act1", "slope1", "x2", "act2", "slope2", "x3", "grads", "outs", "wr", "we", "wg")
+FWD_OUTS = ("inner", "x1", "act1", "slope1", "x2", "act2", "slope2", "x3", "grads", "wr", "we", "wg", "far")
 
 
 def forward_kernel(*refs, images, gather):
     (feat, cotg, m_ref, np_ref, op_ref, wr_in, we_in, wg_in) = refs[:8]
     big = dict(zip(FWD_OUTS, refs[8:21]))
-    n1, n2, n3, norm_all, out_all, sums3 = refs[21:27]
-    (inner, x1, act1, slope1, x2, act2, slope2, x3, grads, land_f, wr, we, wg) = refs[27:40]
-    (land_c, cot, perm, back, z1, ze, col, blocks, st1, st2, st3, st4, send, recv, moves) = refs[40:55]
-    ex1, ex2, ex3, ex4 = (refs[55 + 7 * k : 62 + 7 * k] for k in range(4))
-    held = dict(zip(FWD_OUTS, (inner, x1, act1, slope1, x2, act2, slope2, x3, grads, land_f, wr, we, wg)))
+    block_out, n1, n2, n3, norm_all, out_all, sums3 = refs[21:28]
+    (inner, x1, act1, slope1, x2, act2, slope2, x3, grads, wr, we, wg) = refs[28:40]
+    (land_f, land_c, cot, perm, back, z1, ze, col, blocks, st1, st2, st3, st4, send, recv, moves) = refs[40:56]
+    ex1, ex2, ex3, ex4 = (refs[56 + 7 * k : 63 + 7 * k] for k in range(4))
+    held = dict(zip(FWD_OUTS, (inner, x1, act1, slope1, x2, act2, slope2, x3, grads, wr, we, wg)))
     here = Place()
     grp = here.grp
     rows, own_in = land_f.shape[1:]
@@ -289,8 +291,8 @@
     own_rows = aligned(here.me * rows, rows)
     own_f = links.move(feat.at[own_rows], land_f.at[0], keep=False)
     if gather:
-        wr[here.me, here.line, here.core] = wr_in[...]
-        we[here.me, here.line, here.core] = we_in[...]
+        wr[here.me, here.line, here.core] = wr_in[...].astype(BF16)
+        we[here.me, here.line, here.core] = we_in[...].astype(BF16)
         wg[here.me, here.line, here.core] = wg_in[...]
         loads = []
     else:
@@ -304,8 +306,12 @@
         return [links.send(place, place, peer) for peer in targets]
 
     if gather:
-        wr_a = spread_out(wr, here.across)
-        wg_a = spread_out(wg, here.across)
+        quarter = wr.shape[3] // 4
+        head, rest = pl.ds(0, quarter), pl.ds(quarter, 3 * quarter)
+        half = we.shape[3] // 2
+        lower, upper = pl.ds(0, half), pl.ds(half, half)
+        wr_a = spread_out(wr, here.across, rest)
+        wr_z = spread_out(wr, here.along, head)
     small = []
     for k in range(1, grp):
         peer = here.across[k - 1]
@@ -315,44 +321,49 @@
         small.append(links.send(op_ref, out_all.at[:, span], peer))
     from_f = {}
     for k in range(1, grp):
-        source = feat.at[aligned(here.next_grp(k) * rows, rows)]
-        from_f[grp - k] = links.send(source, land_f.at[grp - k], here.across[k - 1])
+        source = feat.at[aligned(here.partner(k) * rows, rows)]
+        from_f[k] = links.send(source, land_f.at[k], here.across[k - 1])
     own_c = links.move(cotg.at[own_rows], land_c.at[0], keep=False)
     if gather:
         arrived(wr_a)
-        wr_b = [links.send(wr.at[:, here.line, here.core], wr.at[:, here.line, here.core], here.sibling)]
-        wr_l = [links.send(wr.at[:, here.line, here.core], wr.at[:, here.line, here.core], peer) for peer in here.along]
-        arrived(wg_a)
-        wg_b = [links.send(wg.at[:, here.line, here.core], wg.at[:, here.line, here.core], peer) for peer in here.along]
+        place = wr.at[:, here.line, here.core, rest]
+        wr_l = [links.send(place, place, peer) for peer in here.along]
+        wr_b = [links.send(place, place, here.sibling)]
+        arrived(wr_z)
+        place = wr.at[here.me, :, here.core, head]
+        wr_g = [links.send(place, place, peer) for peer in here.across]
+        wg_a = spread_out(wg, here.along)
+        we_a0 = spread_out(we, here.across, lower)
+        we_a1 = spread_out(we, here.along, upper)
     perm[...] = to_inner(rows, images)
     back[...] = to_outer(rows, images)
     own_f.wait()
     for number in range(grp):
         if number:
             from_f[number].wait_recv()
-        span = aligned(here.next_grp(number) * own_in, own_in)
+        span = aligned(here.partner(number) * own_in, own_in)
         inner[:, span] = dot(perm[...], land_f[number]).astype(BF16)
     if gather:
         for k in range(1, here.lines):
             wr_l[k - 1].wait_recv()
-            line = here.next_line(here.lines - k)
-            wr_b.append(links.send(wr.at[:, line, here.core], wr.at[:, line, here.core], here.sibling))
-        arrived(wg_b)
-        wg_c = [links.send(wg.at[:, :, here.core], wg.at[:, :, here.core], here.sibling)]
+            place = wr.at[:, here.next_line(here.lines - k), here.core, rest]
+            wr_b.append(links.send(place, place, here.sibling))
+        arrived(wr_g)
+        place = wr.at[:, :, here.core, head]
+        wr_b.append(links.send(place, place, here.sibling))
+        arrived(wg_a)
+        place = wg.at[here.me, :, here.core]
+        wg_b = [links.send(place, place, peer) for peer in here.across]
+        arrived(we_a0)
+        arrived(we_a1)
+        place = we.at[:, here.line, here.core, lower]
+        we_b = [links.send(place, place, peer) for peer in here.along]
+        place = we.at[here.me, :, here.core, upper]
+        we_b += [links.send(place, place, peer) for peer in here.across]
         arrived(wr_b)
     for copy in loads:
         copy.wait()
     links.move(inner, big["inner"])
-
-    if gather:
-        half = we.shape[3] // 2
-        lower, upper = pl.ds(0, half), pl.ds(half, half)
-        we_a0 = spread_out(we, here.across, lower)
-        we_a1 = spread_out(we, here.along, upper)
-    from_c = {}
-    for k in range(1, grp):
-        source = cotg.at[aligned(here.next_grp(k) * rows, rows)]
-        from_c[grp - k] = links.send(source, land_c.at[grp - k], here.across[k - 1])
 
     steps = width // BLK
 
@@ -364,18 +375,17 @@
 
     links.move(wr, big["wr"])
     if gather:
-        arrived(we_a0)
-        arrived(we_a1)
-        we_b = [
-            links.send(we.at[:, here.line, here.core, lower], we.at[:, here.line, here.core, lower], peer)
-            for peer in here.along
-        ] + [
-            links.send(we.at[here.me, :, here.core, upper], we.at[here.me, :, here.core, upper], peer)
-            for peer in here.across
-        ]
-        arrived(wg_c)
+        arrived(wg_b)
+        place = wg.at[:, :, here.core]
+        wg_c = [links.send(place, place, here.sibling)]
     arrived(small)
     n1[...] = norm_rows(over_devices(st1, ex1, merge_stats))
+    from_c = []
+    for k in range(1, grp):
+        source = cotg.at[aligned(here.partner(k) * rows, rows)]
+        from_c.append(links.send(source, land_c.at[k], here.across[k - 1]))
+    if gather:
+        arrived(wg_c)
 
     clear_edges(col, images, False)
 
@@ -402,7 +412,8 @@
         links.move(held[name], big[name])
     if gather:
         arrived(we_b)
-        we_c = [links.send(we.at[:, :, here.core], we.at[:, :, here.core], here.sibling)]
+        place = we.at[:, :, here.core]
+        we_c = [links.send(place, place, here.sibling)]
     n2[...] = norm_rows(over_devices(st2, ex2, merge_stats))
 
     @pl.loop(0, steps)
@@ -431,11 +442,15 @@
 
     n3[...] = norm_rows(over_devices(st3, ex3, merge_stats))
     own_c.wait()
-    arrived([from_c[number] for number in range(1, grp)])
+    arrived(from_c)
+    to_near = [
+        links.send(land_f.at[k], block_out.at[own_rows], here.across[k - 1], start=False) for k in range(1, grp - 1)
+    ]
 
     @pl.loop(0, grp)
-    def _(number):
-        slot = lax.rem(number + grp - here.me, grp)
+    def _(turn):
+        slot = lax.rem(turn + 1, grp)
+        number = here.partner(slot)
         cot[...] = dot(perm[...], land_c[slot])
         for part in range(0, own_in, BLK):
             span = pl.ds(pl.multiple_of(number * own_in + part, BLK), BLK)
@@ -456,10 +471,18 @@
             st4[0:1, span] = bias_grad
             st4[1:2, span] = gain_grad
         land_f[slot] = dot(back[...], col[:, 0:own_in]).astype(BF16)
-
-    for name in ("x3", "grads", "outs"):
+        for k, copy in enumerate(to_near):
+
+            @pl.when(turn == k)
+            def _():
+                copy.start()
+
+    links.move(land_f.at[0], block_out.at[own_rows])
+    links.move(land_f.at[grp - 1], big["far"])
+    for name in ("x3", "grads"):
         links.move(held[name], big[name])
     sums3[...] = over_devices(st4, ex4, add_rows)
+    arrived(to_near)
     links.close()
 
 
@@ -484,7 +507,7 @@
         "slope2": across,
         "x3": (rows, channels),
         "grads": (rows, channels),
-        "outs": (grp, rows, own_in),
+        "far": (rows, own_in),
         "wr": r_shape,
         "we": e_shape,
         "wg": g_shape,
@@ -499,11 +522,13 @@
     results = pl.pallas_call(
         functools.partial(forward_kernel, images=rows // HW, gather=gather),
         out_shape=[jax.ShapeDtypeStruct(shapes[name], BF16) for name in FWD_OUTS]
+        + [jax.ShapeDtypeStruct(features.shape, BF16)]
         + [jax.ShapeDtypeStruct(shape, F32) for shape in small],
         in_specs=[hbm, hbm, vmem, vmem, vmem] + [vmem if gather else hbm] * 3,
-        out_specs=[hbm] * len(FWD_OUTS) + [vmem] * len(small),
-        scratch_shapes=[pltpu.VMEM(shapes[name], BF16) for name in FWD_OUTS]
+        out_specs=[hbm] * (len(FWD_OUTS) + 1) + [vmem] * len(small),
+        scratch_shapes=[pltpu.VMEM(shapes[name], BF16) for name in FWD_OUTS[:-1]]
         + [
+            pltpu.VMEM((grp, rows, own_in), BF16),
             pltpu.VMEM((grp, rows, own_in), BF16),
             pltpu.VMEM((rows, own_in), F32),
             pltpu.VMEM((rows, rows), BF16),
@@ -526,7 +551,7 @@
         + sums_scratch(2, channels),
         compiler_params=params(collective_id=1, has_side_effects=True),
     )(features, out_cotangent, mask, norm_params, out_params, *weights)
-    return dict(zip(FWD_OUTS, results)), results[len(FWD_OUTS) :]
+    return dict(zip(FWD_OUTS, results)), results[len(FWD_OUTS)], results[len(FWD_OUTS) + 1 :]
 
 
 def packed_groups(weight):
@@ -539,14 +564,18 @@
 
 
 def backward_kernel(*refs, images, owners):
-    outs_in, inner_in = refs[:2]
-    given = dict(zip(BWD_INS, refs[2:13]))
-    m_ref, n1, n2, n3, norm_all, out_all, sums3 = refs[13:20]
-    block_out, input_grad, reduce_out, expand_out, group_out, sums1, sums2 = refs[20:27]
-    (grads, x3, we, act2, slope2, x2, act1, slope1, x1, wg, wr) = refs[27:38]
+    _, far_in, inner_in = refs[:3]
+    given = dict(zip(BWD_INS, refs[3:14]))
+    m_ref, n1, n2, n3, norm_all, out_all, sums3 = refs[14:21]
+    refs = refs[21:]
+    state, refs = (refs[:15], refs[15:]) if owners else ((), refs)
+    block_out, input_grad, reduce_out, expand_out, group_out, sums1, sums2 = refs[:7]
+    raws, refs = ((reduce_out, group_out, expand_out, *refs[7:9]), refs[9:]) if owners else ((), refs[7:])
+    scalars, refs = (refs[0], refs[1:]) if owners else (None, refs)
+    (grads, x3, we, act2, slope2, x2, act1, slope1, x1, wg, wr) = refs[:11]
     held = dict(zip(BWD_INS, (grads, x3, we, act2, slope2, x2, act1, slope1, x1, wg, wr)))
-    (ge, dp, col, blocks, turned, grad_in, back, st1, st2, raw_e, raw_r, raw_g, send, recv, moves) = refs[38:53]
-    ex1, ex2 = refs[53:60], refs[60:67]
+    (ge, dp, col, blocks, turned, grad_in, back, st1, st2, raw_e, raw_r, raw_g, send, recv, moves) = refs[11:26]
+    ex1, ex2 = refs[26:33], refs[33:40]
     here = Place()
     me, grp, core, line, lines = here.me, here.grp, here.core, here.line, here.lines
     rows, width = dp.shape
@@ -556,48 +585,85 @@
     steps = width // BLK
     links = Links(send, recv, moves)
     if owners:
-        (e1, e2, e3, r1, r2, r3, g1, g2, g3, g4, gs1, gs2, gs3) = refs[67:]
+        e_slots, r_slots = refs[40:45], refs[45:50]
+        (g1, g2, g3, g4, gs1, gs2, gs3) = refs[50:57]
+        trust_scratch = refs[57:]
 
     greet(everyone())
     loads = {name: links.move(given[name], held[name], keep=False) for name in BWD_INS}
     own_rows = aligned(me * rows, rows)
-    links.move(outs_in.at[0], block_out.at[own_rows])
     back[...] = to_outer(rows, images)
     greeted(everyone())
-    out_sends = [
-        links.send(outs_in.at[k], block_out.at[own_rows], here.across[k - 1]) for k in range(1, grp)
-    ]
-
-    def core_swap(raw, slot):
-        return links.send(raw.at[:, :, 1 - core], slot, here.sibling)
-
-    def add_core(raw, slot):
+    out_sends = [links.send(far_in, block_out.at[own_rows], here.across[grp - 2])]
+
+    def core_swap(raw, slots):
+        return links.send(raw.at[:, :, 1 - core], slots[0], here.sibling)
+
+    def add_core(raw, slots):
         @pl.loop(0, grp * lines)
         def _(at):
             a, b = at // lines, lax.rem(at, lines)
-            slot[a, b] = (raw[a, b, core].astype(F32) + slot[a, b].astype(F32)).astype(BF16)
-
-    def over_grp(summed, slots):
-        return [links.send(summed.at[here.next_grp(k)], slots.at[k - 1], here.across[k - 1]) for k in range(1, grp)]
-
-    def add_grp(summed, slots):
+            slots[0][a, b] = (raw[a, b, core].astype(F32) + slots[0][a, b].astype(F32)).astype(BF16)
+
+    def halves(slots):
+        half = slots[0].shape[2] // 2
+        return half, pl.ds(0, half), pl.ds(half, half)
+
+    def spread_sums(slots):
+        one, grp_slots, line_slots = slots[:3]
+        _, lower, upper = halves(slots)
+        over = [
+            links.send(one.at[here.partner(k), :, lower], grp_slots.at[k - 1], here.across[k - 1])
+            for k in range(1, grp)
+        ]
+        along = [
+            links.send(one.at[:, here.next_line(k), upper], line_slots.at[k - 1], here.along[k - 1])
+            for k in range(1, lines)
+        ]
+        return over, along
+
+    def add_over(slots):
+        one, grp_slots = slots[:2]
+        half = halves(slots)[0]
+
         @pl.loop(0, lines)
         def _(b):
-            piece = summed[me, b].astype(F32)
+            piece = one[me, b, 0:half].astype(F32)
             for k in range(grp - 1):
-                piece += slots[k, b].astype(F32)
-            slots[0, b] = piece.astype(BF16)
-
-    def over_line(slots, last):
+                piece += grp_slots[k, b].astype(F32)
+            grp_slots[0, b] = piece.astype(BF16)
+
         return [
-            links.send(slots.at[0, here.next_line(k)], last.at[k - 1], here.along[k - 1]) for k in range(1, lines)
+            links.send(grp_slots.at[0, here.next_line(k)], slots[3].at[k - 1], here.along[k - 1])
+            for k in range(1, lines)
         ]
 
-    def add_line(slots, last, out):
-        piece = slots[0, line].astype(F32)
+    def add_along(slots):
+        one, line_slots = slots[0], slots[2]
+        half = halves(slots)[0]
+
+        @pl.loop(0, grp)
+        def _(a):
+            piece = one[a, line, half : 2 * half].astype(F32)
+            for k in range(lines - 1):
+                piece += line_slots[k, a].astype(F32)
+            line_slots[0, a] = piece.astype(BF16)
+
+        return [
+            links.send(line_slots.at[0, here.partner(k)], slots[4].at[k - 1], here.across[k - 1])
+            for k in range(1, grp)
+        ]
+
+    def add_last(slots, out):
+        half, lower, upper = halves(slots)
+        piece = slots[1][0, line].astype(F32)
         for k in range(lines - 1):
-            piece += last[k].astype(F32)
-        out[...] = piece
+            piece += slots[3][k].astype(F32)
+        out[0:half] = piece
+        piece = slots[2][0, me].astype(F32)
+        for k in range(grp - 1):
+            piece += slots[4][k].astype(F32)
+        out[half : 2 * half] = piece
 
     for name in ("grads", "x3", "we", "act2"):
         loads[name].wait()
@@ -639,7 +705,7 @@
                 dp[:, left : left + BLK] += part_sum
 
     if owners:
-        e_core = core_swap(raw_e, e1)
+        e_core = core_swap(raw_e, e_slots)
     else:
         links.move(raw_e, expand_out)
     for name in ("slope2", "x2"):
@@ -663,8 +729,8 @@
     sums2[...] = over_devices(st2, ex2, add_rows)
     if owners:
         e_core.wait_recv()
-        add_core(raw_e, e1)
-        e_grp = over_grp(e1, e2)
+        add_core(raw_e, e_slots)
+        e_over, e_along = spread_sums(e_slots)
 
     for name in ("act1", "slope1", "x1", "wg"):
         loads[name].wait()
@@ -706,16 +772,17 @@
     load_inner = links.move(inner_in, inner, keep=False)
     if owners:
         g_grp = [
-            links.send(raw_g.at[:, aligned(here.next_grp(k) * BLK, BLK)], g1.at[k - 1], here.across[k - 1])
+            links.send(raw_g.at[:, aligned(here.partner(k) * BLK, BLK)], g1.at[k - 1], here.across[k - 1])
             for k in range(1, grp)
         ]
     else:
         links.move(raw_g, group_out)
     sums1[...] = over_devices(st1, ex1, add_rows)
     if owners:
-        arrived(e_grp)
-        add_grp(e1, e2)
-        e_line = over_line(e2, e3)
+        arrived(e_over)
+        e_last = add_over(e_slots)
+        arrived(e_along)
+        e_last += add_along(e_slots)
 
     @pl.loop(0, steps)
     def _(number):
@@ -745,7 +812,7 @@
                 raw_r[number, 0, 0, part : part + BLK] = block
 
     if owners:
-        r_core = core_swap(raw_r, r1)
+        r_core = core_swap(raw_r, r_slots)
         arrived(g_grp)
         total = raw_g[:, aligned(me * BLK, BLK)].astype(F32)
         for k in range(grp - 1):
@@ -754,8 +821,8 @@
         high = line // 2
         g_far = links.send(gs1.at[:, aligned((1 - high) * 128, 128)], g2, here.far)
         r_core.wait_recv()
-        add_core(raw_r, r1)
-        r_grp = over_grp(r1, r2)
+        add_core(raw_r, r_slots)
+        r_over, r_along = spread_sums(r_slots)
     else:
         links.move(raw_r, reduce_out)
     loads["wr"].wait()
@@ -778,30 +845,43 @@
         g_far.wait_recv()
         gs2[...] = (gs1[:, aligned(high * 128, 128)].astype(F32) + g2[...].astype(F32)).astype(BF16)
         g_near = links.send(gs2, g3, here.near)
-        arrived(e_line)
-        add_line(e2, e3, expand_out)
+        arrived(e_last)
+        add_last(e_slots, expand_out)
         g_near.wait_recv()
         gs3[...] = (gs2[...].astype(F32) + g3[...].astype(F32)).astype(BF16)
         g_last = links.send(gs3, g4, here.sibling)
-        g_last.wait_recv()
-        group_out[...] = gs3[...].astype(F32) + g4[...].astype(F32)
-        arrived(r_grp)
-        add_grp(r1, r2)
-        r_line = over_line(r2, r3)
+        arrived(r_over)
+        r_last = add_over(r_slots)
     in_sends = [
-        links.send(grads.at[:, aligned(here.next_grp(k) * own_in, own_in)], input_grad.at[own_rows], here.across[k - 1])
+        links.send(grads.at[:, aligned(here.partner(k) * own_in, own_in)], input_grad.at[own_rows], here.across[k - 1])
         for k in range(1, grp)
     ]
     links.move(grads.at[:, aligned(me * own_in, own_in)], input_grad.at[own_rows])
     if owners:
-        arrived(r_line)
-        add_line(r2, r3, reduce_out)
+        g_last.wait_recv()
+        turned_sum = (gs3[...].astype(F32) + g4[...].astype(F32)).T
+        quarter = lax.rem(here.mine, 4)
+        piece = turned_sum[0:GW]
+        for k in range(1, 4):
+            piece = jnp.where(quarter == k, turned_sum[k * GW : (k + 1) * GW], piece)
+        group_out[...] = piece
+        own_width = width // grp
+        span = aligned(me * own_width, own_width)
+        raws[3][0:1], raws[3][1:2] = sums1[1:2, span], sums1[0:1, span]
+        raws[3][2:3], raws[3][3:4] = sums2[1:2, span], sums2[0:1, span]
+        span = aligned(me * own_in, own_in)
+        raws[4][0:1], raws[4][1:2] = sums3[1:2, span], sums3[0:1, span]
+        arrived(r_along)
+        r_last += add_along(r_slots)
+        arrived(r_last)
+        add_last(r_slots, reduce_out)
+        trust(raws, state[:5], state[5:10], state[10:], scalars, trust_scratch[0], trust_scratch[1:8], trust_scratch[8:])
     arrived(out_sends)
     arrived(in_sends)
     links.close()
 
 
-def backward(kept, mask, n1, n2, n3, norm_all, out_all, sums3, owners):
+def backward(kept, block_out, mask, n1, n2, n3, norm_all, out_all, sums3, state, owners):
     grp = lax.axis_size("grp")
     rows, width = kept["act1"].shape
     channels = kept["x3"].shape[1]
@@ -814,9 +894,15 @@
         parts = [
             jax.ShapeDtypeStruct(r_shape[3:], F32),
             jax.ShapeDtypeStruct(e_shape[3:], F32),
-            jax.ShapeDtypeStruct((9 * GW, 128), F32),
+            jax.ShapeDtypeStruct((GW, 9 * GW), F32),
+        ]
+        last = [
+            jax.ShapeDtypeStruct((4, width // grp), F32),
+            jax.ShapeDtypeStruct((2, own_in), F32),
+            jax.ShapeDtypeStruct((8, 128), F32),
         ]
     else:
+        last = []
         parts = [jax.ShapeDtypeStruct(shape, BF16) for shape in (r_shape, e_shape, (9 * GW, width))]
     sums = [jax.ShapeDtypeStruct((2, width), F32)] * 2
     scratch = [pltpu.VMEM(kept[name].shape, BF16) for name in BWD_INS] + [
@@ -832,32 +918,37 @@
         pltpu.VMEM(e_shape, BF16),
         pltpu.VMEM(r_shape, BF16),
         pltpu.VMEM((9 * GW, width), BF16),
-        pltpu.SemaphoreType.DMA((32,)),
-        pltpu.SemaphoreType.DMA((32,)),
+        pltpu.SemaphoreType.DMA((48,)),
+        pltpu.SemaphoreType.DMA((48,)),
         pltpu.SemaphoreType.DMA((20,)),
     ]
     scratch += sums_scratch(2, width) + sums_scratch(2, width)
     if owners:
         for shape in (e_shape, r_shape):
-            tail = shape[3:]
+            half = (shape[3] // 2, shape[4])
             scratch += [
-                pltpu.VMEM((grp, lines, *tail), BF16),
-                pltpu.VMEM((grp - 1, lines, *tail), BF16),
-                pltpu.VMEM((lines - 1, *tail), BF16),
+                pltpu.VMEM((grp, lines, *shape[3:]), BF16),
+                pltpu.VMEM((grp - 1, lines, *half), BF16),
+                pltpu.VMEM((lines - 1, grp, *half), BF16),
+                pltpu.VMEM((lines - 1, *half), BF16),
+                pltpu.VMEM((grp - 1, *half), BF16),
             ]
         narrow = pltpu.VMEM((9 * GW, 128), BF16)
         scratch += [pltpu.VMEM((grp - 1, 9 * GW, BLK), BF16), narrow, narrow, narrow]
         scratch += [pltpu.VMEM((9 * GW, BLK), BF16), narrow, narrow]
+        scratch += [pltpu.VMEM((2, 8, 128), F32)] + sums_scratch(8, 128) + sums_scratch(8, 128)
     whole = jax.ShapeDtypeStruct((grp * rows, own_in), BF16)
     return pl.pallas_call(
         functools.partial(backward_kernel, images=rows // HW, owners=owners),
-        out_shape=[whole, whole, *parts, *sums],
-        in_specs=[hbm] * 13 + [vmem] * 7,
-        out_specs=[hbm, hbm] + [vmem if owners else hbm] * 3 + [vmem] * 2,
+        out_shape=[whole, whole, *parts, *sums, *last],
+        in_specs=[hbm] * 14 + [vmem] * (7 + len(state)),
+        out_specs=[hbm, hbm] + [vmem if owners else hbm] * 3 + [vmem] * (2 + len(last)),
         scratch_shapes=scratch,
+        input_output_aliases={0: 0},
         compiler_params=params(collective_id=2, has_side_effects=True),
     )(
-        kept["outs"],
+        block_out,
+        kept["far"],
         kept["inner"],
         *[kept[name] for name in BWD_INS],
         mask,
@@ -867,6 +958,7 @@
         norm_all,
         out_all,
         sums3,
+        *state,
     )
 
 
@@ -886,13 +978,9 @@
     return (new_first, new_second, direction)
 
 
-def trust_kernel(*refs):
-    raws, tensors, firsts, seconds = (refs[5 * k : 5 * k + 5] for k in range(4))
-    out_ref, pay, *scratch = refs[20:]
-    one, two = scratch[:7], scratch[7:]
+def trust(raws, tensors, firsts, seconds, out_ref, pay, one, two):
     share = 1.0 / lax.axis_size("batch")
     shares = (1.0, 1.0, 1.0, share, share)
-    greet(everyone())
     square = jnp.zeros((1, 1), F32)
     pay[...] = jnp.zeros_like(pay)
     for number in range(5):
@@ -900,7 +988,6 @@
         weight = shares[number] * whole_sum(tensors[number][...] ** 2)
         pay[0, number + 1 : number + 2] = jnp.broadcast_to(weight, (1, 128))
     pay[0, 0:1] = jnp.broadcast_to(square, (1, 128))
-    greeted(everyone())
     sums = over_devices(pay.at[0], one, add_rows)
     grad_norm = jnp.sqrt(sums[0:1])
     factor = jnp.minimum(1.0, clip_norm / grad_norm)
@@ -921,6 +1008,13 @@
     out_ref[2:7] = jnp.sqrt(sums[1:6]) * lax.rsqrt(steps[1:6] + 1e-06)
 
 
+def trust_kernel(*refs):
+    raws, tensors, firsts, seconds = (refs[5 * k : 5 * k + 5] for k in range(4))
+    greet(everyone())
+    greeted(everyone())
+    trust(raws, tensors, firsts, seconds, refs[20], refs[21], refs[22:29], refs[29:])
+
+
 def update_kernel(*refs):
     scalars = refs[0]
     raws, tensors, firsts, seconds = (refs[5 * k + 1 : 5 * k + 6] for k in range(4))
@@ -941,30 +1035,32 @@
             at += 1
 
 
-def optimizer(raws, tensors, firsts, seconds):
+def trust_alone(raws, state):
     vmem = pl.BlockSpec(memory_space=pltpu.VMEM)
-    state = (*raws, *tensors, *firsts, *seconds)
-    scalars = pl.pallas_call(
+    return pl.pallas_call(
         trust_kernel,
         out_shape=jax.ShapeDtypeStruct((8, 128), F32),
         in_specs=[vmem] * 20,
         out_specs=vmem,
         scratch_shapes=[pltpu.VMEM((2, 8, 128), F32)] + sums_scratch(8, 128) + sums_scratch(8, 128),
-        compiler_params=params(collective_id=8, has_side_effects=True),
-    )(*state)
+        compiler_params=params(collective_id=3, has_side_effects=True),
+    )(*raws, *state)
+
+
+def update(scalars, raws, state):
+    vmem = pl.BlockSpec(memory_space=pltpu.VMEM)
     shapes = []
-    for number, tensor in enumerate(tensors):
+    for number, tensor in enumerate(state[:5]):
         shapes += [jax.ShapeDtypeStruct(tensor.shape, F32)] * 4
         if number < 3:
             shapes.append(jax.ShapeDtypeStruct(tensor.shape, BF16))
-    outs = pl.pallas_call(
+    return pl.pallas_call(
         update_kernel,
         out_shape=shapes,
         in_specs=[vmem] * 21,
         out_specs=[vmem] * len(shapes),
         compiler_params=params(),
-    )(scalars, *state)
-    return scalars, outs
+    )(scalars, *raws, *state)
 
 
 def local(
@@ -989,7 +1085,7 @@
 ):
     grp, batch = lax.axis_size("grp"), lax.axis_size("batch")
     both = ("grp", "batch")
-    me, mine = lax.axis_index("grp"), lax.axis_index("batch")
+    me = lax.axis_index("grp")
     rows = features.shape[0] // grp
     images = rows // HW
     own_in = features.shape[1]
@@ -997,23 +1093,30 @@
     inside = batch == 8 and own_width == 8 * GW
     validity = lax.dynamic_slice_in_dim(pixel_mask, me * rows, rows, 0).astype(F32)
     mask = jnp.broadcast_to(validity.reshape(images, HW).T.reshape(rows, 1), (rows, 128))
-    reduce_w, group_w, expand_w = (value.astype(BF16) for value in (reduce_master, group_master, expand_master))
+    state = (
+        *(reduce_master, group_master.T, expand_master, norm_params, out_params),
+        *(reduce_first, group_first.T, expand_first, norm_first, out_first),
+        *(reduce_second, group_second.T, expand_second, norm_second, out_second),
+    )
+    group_w = group_master.astype(BF16)
     if inside:
+        reduce_w, expand_w = reduce_master, expand_master
         group_w = packed_groups(group_w)[0]
     else:
-        reduce_w = lax.all_gather(reduce_w, both, axis=0, tiled=True)
-        expand_w = lax.all_gather(expand_w, both, axis=0, tiled=True)
+        reduce_w = lax.all_gather(reduce_master.astype(BF16), both, axis=0, tiled=True)
+        expand_w = lax.all_gather(expand_master.astype(BF16), both, axis=0, tiled=True)
         group_w = packed_groups(lax.all_gather(group_w, both, axis=1, tiled=True))
-    kept, (n1, n2, n3, norm_all, out_all, sums_three) = forward(
+    kept, block_out, (n1, n2, n3, norm_all, out_all, sums_three) = forward(
         features, out_cotangent, mask, norm_params, out_params, reduce_w, expand_w, group_w, inside
     )
-    block_out, input_grad, reduce_part, expand_part, group_part, sums_one, sums_two = backward(
-        kept, mask, n1, n2, n3, norm_all, out_all, sums_three, inside
+    block_out, input_grad, reduce_part, expand_part, group_part, sums_one, sums_two, *last = backward(
+        kept, block_out, mask, n1, n2, n3, norm_all, out_all, sums_three, state if inside else (), inside
     )
     if inside:
-        group_part = lax.dynamic_slice_in_dim(group_part, lax.rem(mine, 4) * GW, GW, 1)
+        norm_raw, out_raw, scalars = last
+        raws = (reduce_part, group_part, expand_part, norm_raw, out_raw)
     else:
-        flat = group_part.reshape(9 * GW, grp * batch, -1).transpose(1, 0, 2)
+        flat = group_part.reshape(9 * GW, grp * batch, -1).transpose(1, 2, 0)
         reduce_part, expand_part, group_part = (
             lax.psum_scatter(value, both, scatter_dimension=0).astype(F32)
             for value in (
@@ -1022,17 +1125,14 @@
                 flat,
             )
         )
-    norm_sums = jnp.concatenate([sums_one[1:2], sums_one[0:1], sums_two[1:2], sums_two[0:1]], axis=0)
-    norm_raw = lax.dynamic_slice_in_dim(norm_sums, me * own_width, own_width, 1)
-    out_raw = lax.dynamic_slice_in_dim(
-        jnp.concatenate([sums_three[1:2], sums_three[0:1]], axis=0), me * own_in, own_in, 1
-    )
-    scalars, updates = optimizer(
-        (reduce_part, group_part, expand_part, norm_raw, out_raw),
-        (reduce_master, group_master, expand_master, norm_params, out_params),
-        (reduce_first, group_first, expand_first, norm_first, out_first),
-        (reduce_second, group_second, expand_second, norm_second, out_second),
-    )
+        norm_sums = jnp.concatenate([sums_one[1:2], sums_one[0:1], sums_two[1:2], sums_two[0:1]], axis=0)
+        norm_raw = lax.dynamic_slice_in_dim(norm_sums, me * own_width, own_width, 1)
+        out_sums = jnp.concatenate([sums_three[1:2], sums_three[0:1]], axis=0)
+        out_raw = lax.dynamic_slice_in_dim(out_sums, me * own_in, own_in, 1)
+        raws = (reduce_part, group_part, expand_part, norm_raw, out_raw)
+        scalars = trust_alone(raws, state)
+    updates = list(update(scalars, raws, state))
+    updates[5:10] = [value.T for value in updates[5:10]]
     return (block_out, input_grad, scalars[0, 0], scalars[2:5, 0], scalars[5:7, 0], *updates)
 
 

time: 384 us -> 336 us (0.88)
  Pallas kernels: 356 us -> 322 us
  local copies, waits for them, and re-layouts: 21.5 us -> 12.3 us
  other arithmetic: 5.38 us -> 0.78 us
    pallas_call x2 -> x1, Pallas kernels: 22.7 us -> 3.49 us  [update(): pl.pallas_call(update_kernel, out_shape=shapes, in_specs=[vmem] * 21, out...]
    pallas_call x1, Pallas kernels: 156 us -> 143 us  [backward(): pl.pallas_call(functools.partial(backward_kernel, images=rows // HW, owne...]
    unnamed x24 -> x5, local copies, waits for them, and re-layouts: 15.3 us -> 6.57 us
where the time goes in v2:
time: 336 us
  Pallas kernels  322 us (96%)
  local copies, waits for them, and re-layouts  12.3 us (4%)
    pallas_call x1, Pallas kernels, forward(): pl.pallas_call(functools.partial(forward_kernel, images=rows // HW, gathe...  176 us
    pallas_call x1, Pallas kernels, backward(): pl.pallas_call(functools.partial(backward_kernel, images=rows // HW, owne...  143 us

profile of v2, /device:TPU:0, one launch (start us, length us, event | category | flops | bytes accessed | tf_op | source)
XLA Modules:
  0.0 335.8 jit_solution(3584053140410840346)
XLA Ops:
  0.7 0.8 dynamic-slice_convert_fusion
  1.5 0.1 reshape.67
  1.5 0.1 copy.49
  1.6 0.1 broadcast_in_dim.7
  1.7 0.9 copy.50
  2.7 0.1 copy.51
  2.7 0.7 squeeze_reshape.3.refs_7_
  3.4 0.9 broadcast_in_dim.8.refs_2_.refs_14_
  4.4 175.7 %shard_map.393 = (bf16[784,2048]{1,0:T(8,128)(2,1)}, bf16[784,1024]{1,0:T(8,128)(2,1)}, bf16[784,1024]{1,0:T(8,128)(2,1)}, bf16[784,1024]{1,0:T(8,128)(2,1)}, bf...) custom-call(bf16[3136,512]{1,0:T(8,128)(2,1)} %refs_0_.1, ...), custom_call_target="tpu_custom_call" | custom-call | tf_op jit(solution)/shard_map/pallas_call | solution.py:522
  180.0 142.8 %shard_map.394 = (bf16[3136,512]{1,0:T(8,128)(2,1)}, bf16[3136,512]{1,0:T(8,128)(2,1)}, f32[64,1024]{1,0:T(8,128)}, f32[128,512]{1,0:T(8,128)}, f32[32,288]{1,0:...) custom-call(bf16[3136,512]{1,0:T(8,128)(2,1)} %get-tuple-element.79., ...), custom_call_target="tpu_custom_call", output_to_operand_aliasing={{0}: (0, {})} | custom-call | tf_op jit(solution)/shard_map/pallas_call | solution.py:941
  322.9 1.2 slice.9
  324.1 1.3 slice_reduce_fusion.1
  325.4 1.3 slice_reduce_fusion
  326.7 3.5 %shard_map.395 = (f32[64,1024]{1,0:T(8,128)}, f32[64,1024]{1,0:T(8,128)}, f32[64,1024]{1,0:T(8,128)}, f32[64,1024]{1,0:T(8,128)}, bf16[64,1024]{1,0:T(8,128)(2,1...) custom-call(f32[8,128]{1,0:T(8,128)} %get-tuple-element.101.refs_0_,, ...), custom_call_target="tpu_custom_call" | custom-call | tf_op jit(solution)/shard_map/pallas_call | solution.py:1057
  330.2 0.0 copy-start
  330.2 4.0 %copy.55 = bf16[3136,512]{1,0:T(8,128)(2,1)} copy(bf16[3136,512]{1,0:T(8,128)(2,1)} %get-tuple-element.158) | data formatting | bytes 6422528
  334.1 0.0 copy-done
  334.1 1.7 copy.56
  (1 shorter events, 0.0 us)
Async XLA Ops:
  330.2 4.0 %copy-start = (bf16[3136,512]{1,0:T(8,128)(2,1)S(1)}, bf16[3136,512]{1,0:T(8,128)(2,1)}, u32[]{:S(2)}) copy-start(bf16[3136,512]{1,0:T(8,128)(2,1)} %get-tuple-element.159) | copy-start | bytes 9633796

commit v3 on v2

--- a/solution.py
+++ b/solution.py
@@ -23,7 +23,7 @@
 MESH = pl.DeviceIdType.MESH
 F32 = jnp.float32
 BF16 = jnp.bfloat16
-VMEM_LIMIT = 60 * 1024 * 1024
+VMEM_LIMIT = 62 * 1024 * 1024
 
 
 def params(**more):
@@ -109,10 +109,11 @@
     return jnp.concatenate([total, spread, count], axis=0)
 
 
-def over_devices(source, scratch, merge):
+def over_devices(source, scratch, merge, beside=(None, None)):
     first, second, mid, *sems = scratch
     copies = []
-    for axis, slots, send, recv in (("grp", first, sems[0], sems[1]), ("batch", second, sems[2], sems[3])):
+    levels = (("grp", first, sems[0], sems[1], beside[0]), ("batch", second, sems[2], sems[3], beside[1]))
+    for axis, slots, send, recv, meanwhile in levels:
         here = []
         for number, peer in enumerate(peers(axis)):
             copy = pltpu.make_async_remote_copy(
@@ -120,6 +121,8 @@
             )
             copy.start()
             here.append(copy)
+        if meanwhile is not None:
+            meanwhile()
         for copy in here:
             copy.wait_recv()
         copies += here
@@ -196,6 +199,24 @@
             copy.wait()
 
 
+class Rounds:
+    def __init__(self, rounds):
+        self.rounds, self.at = rounds, 0
+
+    def go(self, count=None):
+        count = len(self.rounds) if count is None else count
+        for copies in self.rounds[self.at : self.at + count]:
+            for copy in copies:
+                copy.start()
+        self.at = min(self.at + count, len(self.rounds))
+
+    def later(self, count=None):
+        return lambda: self.go(count)
+
+    def copies(self, first=0, last=None):
+        return [copy for copies in self.rounds[first:last] for copy in copies]
+
+
 def arrived(copies):
     for copy in copies:
         copy.wait_recv()
@@ -219,6 +240,19 @@
 
     def next_line(self, k):
         return lax.rem(self.line + k, self.lines)
+
+
+def partner_rounds(here, links, rows, part, pair, near=(0, None), far=(0, None)):
+    rounds = []
+    for ks, (first, last) in ((tuple(range(1, here.grp - 1)), near), ((here.grp - 1,), far)):
+        for at in range(0, rows, part)[first:last]:
+            copies = [links.send(*pair(k, pl.ds(at, part)), here.across[k - 1], start=False) for k in ks]
+            rounds.append(copies)
+    return rounds
+
+
+def rows_of(index, rows, span):
+    return pl.ds(pl.multiple_of(index * rows, rows) + span.start, span.size)
 
 
 def aligned(at, size):
@@ -268,6 +302,7 @@
     return pre * masked, masked * (1.0 + pre * (1.0 - sigma))
 
 
+NEAR_ROUNDS = 3
 FWD_OUTS = ("inner", "x1", "act1", "slope1", "x2", "act2", "slope2", "x3", "grads", "wr", "we", "wg", "far")
 
 
@@ -356,10 +391,27 @@
         wg_b = [links.send(place, place, peer) for peer in here.across]
         arrived(we_a0)
         arrived(we_a1)
-        place = we.at[:, here.line, here.core, lower]
-        we_b = [links.send(place, place, peer) for peer in here.along]
-        place = we.at[here.me, :, here.core, upper]
-        we_b += [links.send(place, place, peer) for peer in here.across]
+        we_z = Rounds(
+            [
+                [
+                    links.send(
+                        we.at[a, here.line, here.core, lower], we.at[a, here.line, here.core, lower], peer, start=False
+                    )
+                    for peer in here.along
+                ]
+                for a in range(grp)
+            ]
+        )
+        we_g = Rounds(
+            [
+                [
+                    links.send(we.at[here.me, b, here.core, upper], we.at[here.me, b, here.core, upper], peer, start=False)
+                    for peer in here.across
+                ]
+                for b in range(here.lines)
+            ]
+        )
+        we_z.go(1)
         arrived(wr_b)
     for copy in loads:
         copy.wait()
@@ -374,18 +426,34 @@
         block_stats(z1, number * BLK, BLK, m_ref, st1, step)
 
     links.move(wr, big["wr"])
+    arrived(small)
+    from_c = Rounds(
+        partner_rounds(
+            here,
+            links,
+            rows,
+            step,
+            lambda k, span: (cotg.at[rows_of(here.partner(k), rows, span)], land_c.at[k, span]),
+        )
+    )
+    wg_c = []
+
+    def groups_on():
+        if gather:
+            arrived(wg_b)
+            place = wg.at[:, :, here.core]
+            wg_c.append(links.send(place, place, here.sibling))
+            we_g.go(1)
+            we_z.go(2)
+
+    def expand_on():
+        if gather:
+            we_g.go(1)
+
+    n1[...] = norm_rows(over_devices(st1, ex1, merge_stats, (expand_on, groups_on)))
+    arrived(wg_c)
     if gather:
-        arrived(wg_b)
-        place = wg.at[:, :, here.core]
-        wg_c = [links.send(place, place, here.sibling)]
-    arrived(small)
-    n1[...] = norm_rows(over_devices(st1, ex1, merge_stats))
-    from_c = []
-    for k in range(1, grp):
-        source = cotg.at[aligned(here.partner(k) * rows, rows)]
-        from_c.append(links.send(source, land_c.at[k], here.across[k - 1]))
-    if gather:
-        arrived(wg_c)
+        we_g.go()
 
     clear_edges(col, images, False)
 
@@ -411,10 +479,20 @@
     for name in ("x1", "act1", "slope1", "wg"):
         links.move(held[name], big[name])
     if gather:
-        arrived(we_b)
-        place = we.at[:, :, here.core]
+        arrived(we_g.copies())
+        arrived(we_z.copies(0, 3))
+        place = we.at[:, :, here.core, upper]
         we_c = [links.send(place, place, here.sibling)]
-    n2[...] = norm_rows(over_devices(st2, ex2, merge_stats))
+        place = we.at[0 : grp - 1, :, here.core, lower]
+        we_c.append(links.send(place, place, here.sibling))
+
+    def expand_last():
+        if gather:
+            we_z.go()
+        from_c.go(1)
+
+    n2[...] = norm_rows(over_devices(st2, ex2, merge_stats, (from_c.later(1), expand_last)))
+    from_c.go(2)
 
     @pl.loop(0, steps)
     def _(number):
@@ -429,7 +507,11 @@
 
     for name in ("x2", "act2", "slope2"):
         links.move(held[name], big[name])
+    from_c.go(3)
     if gather:
+        arrived(we_z.copies(3))
+        place = we.at[grp - 1, :, here.core, lower]
+        we_c.append(links.send(place, place, here.sibling))
         arrived(we_c)
     links.move(we, big["we"])
 
@@ -440,16 +522,24 @@
             ze[:, span] = dot(act2[...], we[number, :, :, :, part : part + BLK].reshape(width, BLK))
         block_stats(ze, number * own_in, own_in, m_ref, st3, step)
 
-    n3[...] = norm_rows(over_devices(st3, ex3, merge_stats))
+    n3[...] = norm_rows(over_devices(st3, ex3, merge_stats, (from_c.later(1), from_c.later(1))))
+    from_c.go()
     own_c.wait()
-    arrived(from_c)
-    to_near = [
-        links.send(land_f.at[k], block_out.at[own_rows], here.across[k - 1], start=False) for k in range(1, grp - 1)
-    ]
-
-    @pl.loop(0, grp)
-    def _(turn):
-        slot = lax.rem(turn + 1, grp)
+    to_near = Rounds(
+        partner_rounds(
+            here,
+            links,
+            rows,
+            step,
+            lambda k, span: (land_f.at[k, span], block_out.at[rows_of(here.me, rows, span)]),
+            near=(0, NEAR_ROUNDS),
+            far=(0, 0),
+        )
+    )
+    parts = SIDE
+    arrived(from_c.copies(0, parts))
+
+    def output_block(slot):
         number = here.partner(slot)
         cot[...] = dot(perm[...], land_c[slot])
         for part in range(0, own_in, BLK):
@@ -471,18 +561,17 @@
             st4[0:1, span] = bias_grad
             st4[1:2, span] = gain_grad
         land_f[slot] = dot(back[...], col[:, 0:own_in]).astype(BF16)
-        for k, copy in enumerate(to_near):
-
-            @pl.when(turn == k)
-            def _():
-                copy.start()
-
+
+    pl.loop(0, grp - 1)(output_block)
+    to_near.go(1)
+    arrived(from_c.copies(parts))
+    output_block(grp - 1)
     links.move(land_f.at[0], block_out.at[own_rows])
-    links.move(land_f.at[grp - 1], big["far"])
+    links.move(land_f.at[1:], big["far"])
     for name in ("x3", "grads"):
         links.move(held[name], big[name])
-    sums3[...] = over_devices(st4, ex4, add_rows)
-    arrived(to_near)
+    sums3[...] = over_devices(st4, ex4, add_rows, (to_near.later(1), to_near.later()))
+    arrived(to_near.copies())
     links.close()
 
 
@@ -507,7 +596,7 @@
         "slope2": across,
         "x3": (rows, channels),
         "grads": (rows, channels),
-        "far": (rows, own_in),
+        "far": (grp - 1, rows, own_in),
         "wr": r_shape,
         "we": e_shape,
         "wg": g_shape,
@@ -541,8 +630,8 @@
             pltpu.VMEM((3, width), F32),
             pltpu.VMEM((3, channels), F32),
             pltpu.VMEM((2, channels), F32),
-            pltpu.SemaphoreType.DMA((64,)),
-            pltpu.SemaphoreType.DMA((64,)),
+            pltpu.SemaphoreType.DMA((112,)),
+            pltpu.SemaphoreType.DMA((112,)),
             pltpu.SemaphoreType.DMA((20,)),
         ]
         + sums_scratch(3, width)
@@ -590,14 +679,33 @@
         trust_scratch = refs[57:]
 
     greet(everyone())
-    loads = {name: links.move(given[name], held[name], keep=False) for name in BWD_INS}
+    loads = {name: links.move(given[name], held[name], keep=False) for name in BWD_INS[:4]}
     own_rows = aligned(me * rows, rows)
     back[...] = to_outer(rows, images)
     greeted(everyone())
-    out_sends = [links.send(far_in, block_out.at[own_rows], here.across[grp - 2])]
+    to_out = Rounds(
+        partner_rounds(
+            here,
+            links,
+            rows,
+            step,
+            lambda k, span: (far_in.at[k - 1, span], block_out.at[rows_of(me, rows, span)]),
+            near=(NEAR_ROUNDS, None),
+        )
+    )
+    to_out.go(7)
 
     def core_swap(raw, slots):
-        return links.send(raw.at[:, :, 1 - core], slots[0], here.sibling)
+        return [
+            links.send(raw.at[a, :, 1 - core], slots[0].at[a], here.sibling, start=False) for a in range(grp)
+        ]
+
+    def swap_now(copies, number):
+        for a, copy in enumerate(copies):
+
+            @pl.when(number == a)
+            def _():
+                copy.start()
 
     def add_core(raw, slots):
         @pl.loop(0, grp * lines)
@@ -605,13 +713,13 @@
             a, b = at // lines, lax.rem(at, lines)
             slots[0][a, b] = (raw[a, b, core].astype(F32) + slots[0][a, b].astype(F32)).astype(BF16)
 
-    def halves(slots):
-        half = slots[0].shape[2] // 2
-        return half, pl.ds(0, half), pl.ds(half, half)
+    def cuts(slots):
+        cut, rest = slots[1].shape[2], slots[2].shape[2]
+        return cut, pl.ds(0, cut), pl.ds(cut, rest)
 
     def spread_sums(slots):
         one, grp_slots, line_slots = slots[:3]
-        _, lower, upper = halves(slots)
+        _, lower, upper = cuts(slots)
         over = [
             links.send(one.at[here.partner(k), :, lower], grp_slots.at[k - 1], here.across[k - 1])
             for k in range(1, grp)
@@ -624,11 +732,11 @@
 
     def add_over(slots):
         one, grp_slots = slots[:2]
-        half = halves(slots)[0]
+        cut = cuts(slots)[0]
 
         @pl.loop(0, lines)
         def _(b):
-            piece = one[me, b, 0:half].astype(F32)
+            piece = one[me, b, 0:cut].astype(F32)
             for k in range(grp - 1):
                 piece += grp_slots[k, b].astype(F32)
             grp_slots[0, b] = piece.astype(BF16)
@@ -640,11 +748,11 @@
 
     def add_along(slots):
         one, line_slots = slots[0], slots[2]
-        half = halves(slots)[0]
+        cut = cuts(slots)[0]
 
         @pl.loop(0, grp)
         def _(a):
-            piece = one[a, line, half : 2 * half].astype(F32)
+            piece = one[a, line, cut:].astype(F32)
             for k in range(lines - 1):
                 piece += line_slots[k, a].astype(F32)
             line_slots[0, a] = piece.astype(BF16)
@@ -655,18 +763,21 @@
         ]
 
     def add_last(slots, out):
-        half, lower, upper = halves(slots)
+        cut = cuts(slots)[0]
         piece = slots[1][0, line].astype(F32)
         for k in range(lines - 1):
             piece += slots[3][k].astype(F32)
-        out[0:half] = piece
+        out[0:cut] = piece
         piece = slots[2][0, me].astype(F32)
         for k in range(grp - 1):
             piece += slots[4][k].astype(F32)
-        out[half : 2 * half] = piece
-
-    for name in ("grads", "x3", "we", "act2"):
+        out[cut:] = piece
+
+    for name in BWD_INS[:4]:
         loads[name].wait()
+    loads.update({name: links.move(given[name], held[name], keep=False) for name in BWD_INS[4:]})
+    if owners:
+        e_core = core_swap(raw_e, e_slots)
 
     @pl.loop(0, grp)
     def _(number):
@@ -704,9 +815,10 @@
             def _():
                 dp[:, left : left + BLK] += part_sum
 
-    if owners:
-        e_core = core_swap(raw_e, e_slots)
-    else:
+        if owners:
+            swap_now(e_core, number)
+
+    if not owners:
         links.move(raw_e, expand_out)
     for name in ("slope2", "x2"):
         loads[name].wait()
@@ -726,9 +838,9 @@
             sums[1:2, span] = gain_grad
 
     norm_sums(slope2, x2, st2)
-    sums2[...] = over_devices(st2, ex2, add_rows)
+    sums2[...] = over_devices(st2, ex2, add_rows, (to_out.later(1), to_out.later(1)))
     if owners:
-        e_core.wait_recv()
+        arrived(e_core)
         add_core(raw_e, e_slots)
         e_over, e_along = spread_sums(e_slots)
 
@@ -770,19 +882,25 @@
     norm_sums(slope1, x1, st1)
     inner = col.at[:, 0:channels]
     load_inner = links.move(inner_in, inner, keep=False)
-    if owners:
-        g_grp = [
-            links.send(raw_g.at[:, aligned(here.partner(k) * BLK, BLK)], g1.at[k - 1], here.across[k - 1])
-            for k in range(1, grp)
-        ]
-    else:
+    g_grp = []
+
+    def groups_on():
+        if owners:
+            g_grp.extend(
+                links.send(raw_g.at[:, aligned(here.partner(k) * BLK, BLK)], g1.at[k - 1], here.across[k - 1])
+                for k in range(1, grp)
+            )
+
+    if not owners:
         links.move(raw_g, group_out)
-    sums1[...] = over_devices(st1, ex1, add_rows)
+    sums1[...] = over_devices(st1, ex1, add_rows, (to_out.later(1), groups_on))
     if owners:
         arrived(e_over)
         e_last = add_over(e_slots)
         arrived(e_along)
         e_last += add_along(e_slots)
+        r_core = core_swap(raw_r, r_slots)
+    to_out.go()
 
     @pl.loop(0, steps)
     def _(number):
@@ -810,9 +928,13 @@
                     raw_r[number, b, c] = block[k * per_r : (k + 1) * per_r]
             else:
                 raw_r[number, 0, 0, part : part + BLK] = block
+        if owners:
+            swap_now(r_core, number)
 
     if owners:
-        r_core = core_swap(raw_r, r_slots)
+        arrived(r_core)
+        add_core(raw_r, r_slots)
+        r_over, r_along = spread_sums(r_slots)
         arrived(g_grp)
         total = raw_g[:, aligned(me * BLK, BLK)].astype(F32)
         for k in range(grp - 1):
@@ -820,9 +942,6 @@
         gs1[...] = total.astype(BF16)
         high = line // 2
         g_far = links.send(gs1.at[:, aligned((1 - high) * 128, 128)], g2, here.far)
-        r_core.wait_recv()
-        add_core(raw_r, r_slots)
-        r_over, r_along = spread_sums(r_slots)
     else:
         links.move(raw_r, reduce_out)
     loads["wr"].wait()
@@ -841,7 +960,21 @@
             ge[:, part : part + BLK] = total.astype(BF16)
         grads[:, aligned(number * own_in, own_in)] = dot(back[...], ge[...]).astype(BF16)
 
+    to_in = Rounds(
+        partner_rounds(
+            here,
+            links,
+            rows,
+            step,
+            lambda k, span: (
+                grads.at[span, aligned(here.partner(k) * own_in, own_in)],
+                input_grad.at[rows_of(me, rows, span)],
+            ),
+        )
+    )
+    links.move(grads.at[:, aligned(me * own_in, own_in)], input_grad.at[own_rows])
     if owners:
+        to_in.go(4)
         g_far.wait_recv()
         gs2[...] = (gs1[:, aligned(high * 128, 128)].astype(F32) + g2[...].astype(F32)).astype(BF16)
         g_near = links.send(gs2, g3, here.near)
@@ -850,14 +983,12 @@
         g_near.wait_recv()
         gs3[...] = (gs2[...].astype(F32) + g3[...].astype(F32)).astype(BF16)
         g_last = links.send(gs3, g4, here.sibling)
-        arrived(r_over)
-        r_last = add_over(r_slots)
-    in_sends = [
-        links.send(grads.at[:, aligned(here.partner(k) * own_in, own_in)], input_grad.at[own_rows], here.across[k - 1])
-        for k in range(1, grp)
-    ]
-    links.move(grads.at[:, aligned(me * own_in, own_in)], input_grad.at[own_rows])
-    if owners:
+        own_width = width // grp
+        span = aligned(me * own_width, own_width)
+        raws[3][0:1], raws[3][1:2] = sums1[1:2, span], sums1[0:1, span]
+        raws[3][2:3], raws[3][3:4] = sums2[1:2, span], sums2[0:1, span]
+        span = aligned(me * own_in, own_in)
+        raws[4][0:1], raws[4][1:2] = sums3[1:2, span], sums3[0:1, span]
         g_last.wait_recv()
         turned_sum = (gs3[...].astype(F32) + g4[...].astype(F32)).T
         quarter = lax.rem(here.mine, 4)
@@ -865,19 +996,29 @@
         for k in range(1, 4):
             piece = jnp.where(quarter == k, turned_sum[k * GW : (k + 1) * GW], piece)
         group_out[...] = piece
-        own_width = width // grp
-        span = aligned(me * own_width, own_width)
-        raws[3][0:1], raws[3][1:2] = sums1[1:2, span], sums1[0:1, span]
-        raws[3][2:3], raws[3][3:4] = sums2[1:2, span], sums2[0:1, span]
-        span = aligned(me * own_in, own_in)
-        raws[4][0:1], raws[4][1:2] = sums3[1:2, span], sums3[0:1, span]
+        arrived(r_over)
+        r_last = add_over(r_slots)
         arrived(r_along)
         r_last += add_along(r_slots)
+        to_in.go(1)
         arrived(r_last)
         add_last(r_slots, reduce_out)
-        trust(raws, state[:5], state[5:10], state[10:], scalars, trust_scratch[0], trust_scratch[1:8], trust_scratch[8:])
-    arrived(out_sends)
-    arrived(in_sends)
+        beside = (to_in.later(1), to_in.later(1), to_in.later(1), to_in.later())
+        trust(
+            raws,
+            state[:5],
+            state[5:10],
+            state[10:],
+            scalars,
+            trust_scratch[0],
+            trust_scratch[1:8],
+            trust_scratch[8:],
+            beside,
+        )
+    else:
+        to_in.go()
+    arrived(to_out.copies())
+    arrived(to_in.copies())
     links.close()
 
 
@@ -918,20 +1059,20 @@
         pltpu.VMEM(e_shape, BF16),
         pltpu.VMEM(r_shape, BF16),
         pltpu.VMEM((9 * GW, width), BF16),
-        pltpu.SemaphoreType.DMA((48,)),
-        pltpu.SemaphoreType.DMA((48,)),
+        pltpu.SemaphoreType.DMA((96,)),
+        pltpu.SemaphoreType.DMA((96,)),
         pltpu.SemaphoreType.DMA((20,)),
     ]
     scratch += sums_scratch(2, width) + sums_scratch(2, width)
     if owners:
         for shape in (e_shape, r_shape):
-            half = (shape[3] // 2, shape[4])
+            cut = shape[3] * 5 // 128 * 16 if shape[3] > 64 else shape[3] // 2
             scratch += [
                 pltpu.VMEM((grp, lines, *shape[3:]), BF16),
-                pltpu.VMEM((grp - 1, lines, *half), BF16),
-                pltpu.VMEM((lines - 1, grp, *half), BF16),
-                pltpu.VMEM((lines - 1, *half), BF16),
-                pltpu.VMEM((grp - 1, *half), BF16),
+                pltpu.VMEM((grp - 1, lines, cut, shape[4]), BF16),
+                pltpu.VMEM((lines - 1, grp, shape[3] - cut, shape[4]), BF16),
+                pltpu.VMEM((lines - 1, cut, shape[4]), BF16),
+                pltpu.VMEM((grp - 1, shape[3] - cut, shape[4]), BF16),
             ]
         narrow = pltpu.VMEM((9 * GW, 128), BF16)
         scratch += [pltpu.VMEM((grp - 1, 9 * GW, BLK), BF16), narrow, narrow, narrow]
@@ -978,7 +1119,7 @@
     return (new_first, new_second, direction)
 
 
-def trust(raws, tensors, firsts, seconds, out_ref, pay, one, two):
+def trust(raws, tensors, firsts, seconds, out_ref, pay, one, two, beside=(None,) * 4):
     share = 1.0 / lax.axis_size("batch")
     shares = (1.0, 1.0, 1.0, share, share)
     square = jnp.zeros((1, 1), F32)
@@ -988,7 +1129,7 @@
         weight = shares[number] * whole_sum(tensors[number][...] ** 2)
         pay[0, number + 1 : number + 2] = jnp.broadcast_to(weight, (1, 128))
     pay[0, 0:1] = jnp.broadcast_to(square, (1, 128))
-    sums = over_devices(pay.at[0], one, add_rows)
+    sums = over_devices(pay.at[0], one, add_rows, beside[:2])
     grad_norm = jnp.sqrt(sums[0:1])
     factor = jnp.minimum(1.0, clip_norm / grad_norm)
     for number in range(5):
@@ -1001,7 +1142,7 @@
         )[2]
         step = shares[number] * whole_sum(direction * direction)
         pay[1, number + 1 : number + 2] = jnp.broadcast_to(step, (1, 128))
-    steps = over_devices(pay.at[1], two, add_rows)
+    steps = over_devices(pay.at[1], two, add_rows, beside[2:])
     out_ref[...] = jnp.zeros_like(out_ref)
     out_ref[0:1] = grad_norm
     out_ref[1:2] = factor

time: 336 us -> 293 us (0.87)
  Pallas kernels: 322 us -> 279 us
    pallas_call x1, Pallas kernels: 176 us -> 142 us  [forward(): pl.pallas_call(functools.partial(forward_kernel, images=rows // HW, gathe...]
    pallas_call x1, Pallas kernels: 143 us -> 133 us  [backward(): pl.pallas_call(functools.partial(backward_kernel, images=rows // HW, owne...]
where the time goes in v3:
time: 293 us
  Pallas kernels  279 us (95%)
  local copies, waits for them, and re-layouts  12.3 us (4%)
    pallas_call x1, Pallas kernels, forward(): pl.pallas_call(functools.partial(forward_kernel, images=rows // HW, gathe...  142 us
    pallas_call x1, Pallas kernels, backward(): pl.pallas_call(functools.partial(backward_kernel, images=rows // HW, owne...  133 us
    unnamed x5, local copies, waits for them, and re-layouts  6.57 us

profile of v3, /device:TPU:0, one launch (start us, length us, event | category | flops | bytes accessed | tf_op | source)
XLA Modules:
  0.0 292.6 jit_solution(12973724639891451541)
XLA Ops:
  0.7 0.8 dynamic-slice_convert_fusion
  1.5 0.1 reshape.67
  1.5 0.1 copy.49
  1.6 0.1 broadcast_in_dim.7
  1.7 0.9 copy.50
  2.7 0.1 copy.51
  2.7 0.7 squeeze_reshape.3.refs_7_
  3.4 0.9 broadcast_in_dim.8.refs_2_.refs_14_
  4.4 142.3 %shard_map.393 = (bf16[784,2048]{1,0:T(8,128)(2,1)}, bf16[784,1024]{1,0:T(8,128)(2,1)}, bf16[784,1024]{1,0:T(8,128)(2,1)}, bf16[784,1024]{1,0:T(8,128)(2,1)}, bf...) custom-call(bf16[3136,512]{1,0:T(8,128)(2,1)} %refs_0_.1, ...), custom_call_target="tpu_custom_call" | custom-call | tf_op jit(solution)/shard_map/pallas_call | solution.py:611
  146.7 133.0 %shard_map.394 = (bf16[3136,512]{1,0:T(8,128)(2,1)}, bf16[3136,512]{1,0:T(8,128)(2,1)}, f32[64,1024]{1,0:T(8,128)}, f32[128,512]{1,0:T(8,128)}, f32[32,288]{1,0:...) custom-call(bf16[3136,512]{1,0:T(8,128)(2,1)} %get-tuple-element.79., ...), custom_call_target="tpu_custom_call", output_to_operand_aliasing={{0}: (0, {})} | custom-call | tf_op jit(solution)/shard_map/pallas_call | solution.py:1082
  279.7 1.2 slice.9
  280.9 1.3 slice_reduce_fusion.1
  282.2 1.3 slice_reduce_fusion
  283.5 3.5 %shard_map.395 = (f32[64,1024]{1,0:T(8,128)}, f32[64,1024]{1,0:T(8,128)}, f32[64,1024]{1,0:T(8,128)}, f32[64,1024]{1,0:T(8,128)}, bf16[64,1024]{1,0:T(8,128)(2,1...) custom-call(f32[8,128]{1,0:T(8,128)} %get-tuple-element.101.refs_0_,, ...), custom_call_target="tpu_custom_call" | custom-call | tf_op jit(solution)/shard_map/pallas_call | solution.py:1198
  287.0 0.0 copy-start
  287.0 4.0 %copy.55 = bf16[3136,512]{1,0:T(8,128)(2,1)} copy(bf16[3136,512]{1,0:T(8,128)(2,1)} %get-tuple-element.158) | data formatting | bytes 6422528
  290.9 0.0 copy-done
  290.9 1.7 copy.56
  (1 shorter events, 0.0 us)
Async XLA Ops:
  287.0 4.0 %copy-start = (bf16[3136,512]{1,0:T(8,128)(2,1)S(1)}, bf16[3136,512]{1,0:T(8,128)(2,1)}, u32[]{:S(2)}) copy-start(bf16[3136,512]{1,0:T(8,128)(2,1)} %get-tuple-element.159) | copy-start | bytes 9633796

commit v4 on v3

--- a/solution.py
+++ b/solution.py
@@ -326,9 +326,16 @@
     own_rows = aligned(here.me * rows, rows)
     own_f = links.move(feat.at[own_rows], land_f.at[0], keep=False)
     if gather:
-        wr[here.me, here.line, here.core] = wr_in[...].astype(BF16)
-        we[here.me, here.line, here.core] = we_in[...].astype(BF16)
-        wg[here.me, here.line, here.core] = wg_in[...]
+        shard_r, shard_e = refs[84:86]
+        shards = [
+            links.move(wr_in, shard_r, keep=False),
+            links.move(we_in, shard_e, keep=False),
+            links.move(wg_in, wg.at[here.me, here.line, here.core], keep=False),
+        ]
+        for copy in shards:
+            copy.wait()
+        wr[here.me, here.line, here.core] = shard_r[...].astype(BF16)
+        we[here.me, here.line, here.core] = shard_e[...].astype(BF16)
         loads = []
     else:
         loads = [links.move(wr_in, wr, keep=False), links.move(we_in, we, keep=False), links.move(wg_in, wg, keep=False)]
@@ -412,6 +419,7 @@
             ]
         )
         we_z.go(1)
+        we_g.go(1)
         arrived(wr_b)
     for copy in loads:
         copy.wait()
@@ -454,6 +462,7 @@
     arrived(wg_c)
     if gather:
         we_g.go()
+    from_c.go(1)
 
     clear_edges(col, images, False)
 
@@ -489,9 +498,9 @@
     def expand_last():
         if gather:
             we_z.go()
-        from_c.go(1)
-
-    n2[...] = norm_rows(over_devices(st2, ex2, merge_stats, (from_c.later(1), expand_last)))
+        from_c.go(2)
+
+    n2[...] = norm_rows(over_devices(st2, ex2, merge_stats, (from_c.later(2), expand_last)))
     from_c.go(2)
 
     @pl.loop(0, steps)
@@ -613,7 +622,7 @@
         out_shape=[jax.ShapeDtypeStruct(shapes[name], BF16) for name in FWD_OUTS]
         + [jax.ShapeDtypeStruct(features.shape, BF16)]
         + [jax.ShapeDtypeStruct(shape, F32) for shape in small],
-        in_specs=[hbm, hbm, vmem, vmem, vmem] + [vmem if gather else hbm] * 3,
+        in_specs=[hbm, hbm, vmem, vmem, vmem] + [hbm] * 3,
         out_specs=[hbm] * (len(FWD_OUTS) + 1) + [vmem] * len(small),
         scratch_shapes=[pltpu.VMEM(shapes[name], BF16) for name in FWD_OUTS[:-1]]
         + [
@@ -632,12 +641,13 @@
             pltpu.VMEM((2, channels), F32),
             pltpu.SemaphoreType.DMA((112,)),
             pltpu.SemaphoreType.DMA((112,)),
-            pltpu.SemaphoreType.DMA((20,)),
+            pltpu.SemaphoreType.DMA((24,)),
         ]
         + sums_scratch(3, width)
         + sums_scratch(3, width)
         + sums_scratch(3, channels)
-        + sums_scratch(2, channels),
+        + sums_scratch(2, channels)
+        + ([pltpu.VMEM(reduce_w.shape, F32), pltpu.VMEM(expand_w.shape, F32)] if gather else []),
         compiler_params=params(collective_id=1, has_side_effects=True),
     )(features, out_cotangent, mask, norm_params, out_params, *weights)
     return dict(zip(FWD_OUTS, results)), results[len(FWD_OUTS)], results[len(FWD_OUTS) + 1 :]
@@ -676,7 +686,8 @@
     if owners:
         e_slots, r_slots = refs[40:45], refs[45:50]
         (g1, g2, g3, g4, gs1, gs2, gs3) = refs[50:57]
-        trust_scratch = refs[57:]
+        trust_scratch = refs[57:72]
+        state_in, state = state, refs[72:]
 
     greet(everyone())
     loads = {name: links.move(given[name], held[name], keep=False) for name in BWD_INS[:4]}
@@ -777,6 +788,7 @@
         loads[name].wait()
     loads.update({name: links.move(given[name], held[name], keep=False) for name in BWD_INS[4:]})
     if owners:
+        state_loads = [links.move(source, target, keep=False) for source, target in zip(state_in, state)]
         e_core = core_swap(raw_e, e_slots)
 
     @pl.loop(0, grp)
@@ -974,7 +986,7 @@
     )
     links.move(grads.at[:, aligned(me * own_in, own_in)], input_grad.at[own_rows])
     if owners:
-        to_in.go(4)
+        to_in.go(7)
         g_far.wait_recv()
         gs2[...] = (gs1[:, aligned(high * 128, 128)].astype(F32) + g2[...].astype(F32)).astype(BF16)
         g_near = links.send(gs2, g3, here.near)
@@ -1000,10 +1012,12 @@
         r_last = add_over(r_slots)
         arrived(r_along)
         r_last += add_along(r_slots)
-        to_in.go(1)
+        to_in.go(2)
         arrived(r_last)
         add_last(r_slots, reduce_out)
-        beside = (to_in.later(1), to_in.later(1), to_in.later(1), to_in.later())
+        for copy in state_loads:
+            copy.wait()
+        beside = (to_in.later(1), to_in.later(2), to_in.later(1), to_in.later())
         trust(
             raws,
             state[:5],
@@ -1061,7 +1075,7 @@
         pltpu.VMEM((9 * GW, width), BF16),
         pltpu.SemaphoreType.DMA((96,)),
         pltpu.SemaphoreType.DMA((96,)),
-        pltpu.SemaphoreType.DMA((20,)),
+        pltpu.SemaphoreType.DMA((40,)),
     ]
     scratch += sums_scratch(2, width) + sums_scratch(2, width)
     if owners:
@@ -1078,11 +1092,12 @@
         scratch += [pltpu.VMEM((grp - 1, 9 * GW, BLK), BF16), narrow, narrow, narrow]
         scratch += [pltpu.VMEM((9 * GW, BLK), BF16), narrow, narrow]
         scratch += [pltpu.VMEM((2, 8, 128), F32)] + sums_scratch(8, 128) + sums_scratch(8, 128)
+        scratch += [pltpu.VMEM(value.shape, F32) for value in state]
     whole = jax.ShapeDtypeStruct((grp * rows, own_in), BF16)
     return pl.pallas_call(
         functools.partial(backward_kernel, images=rows // HW, owners=owners),
         out_shape=[whole, whole, *parts, *sums, *last],
-        in_specs=[hbm] * 14 + [vmem] * (7 + len(state)),
+        in_specs=[hbm] * 14 + [vmem] * 7 + [hbm] * len(state),
         out_specs=[hbm, hbm] + [vmem if owners else hbm] * 3 + [vmem] * (2 + len(last)),
         scratch_shapes=scratch,
         input_output_aliases={0: 0},
@@ -1157,23 +1172,44 @@
 
 
 def update_kernel(*refs):
-    scalars = refs[0]
-    raws, tensors, firsts, seconds = (refs[5 * k + 1 : 5 * k + 6] for k in range(4))
-    outs = refs[21:]
+    scalars, results = refs[0], refs[1:3]
+    raws, tensors, firsts, seconds = (refs[5 * k + 3 : 5 * k + 8] for k in range(4))
+    norm_out, weight_out, rows_out, *refs = refs[23:]
+    targets, outs, rooms, sems = refs[:2], refs[2:-3], refs[-3:-1], refs[-1]
+    copies, onward = [], []
+    for number, (source, room, target) in enumerate(zip(results, rooms, targets)):
+        part = source.shape[0] // 4
+        for at in range(4):
+            span = pl.ds(at * part, part)
+            copies.append(pltpu.make_async_copy(source.at[span], room.at[span], sems.at[0, number, at]))
+            onward.append(pltpu.make_async_copy(room.at[span], target.at[span], sems.at[1, number, at]))
+            copies[-1].start()
+    norm_out[0] = scalars[0, 0]
     at = 0
     for number in range(5):
-        clipped = scalars[1:2, 0:1] * raws[number][...]
+        trust_ratio = scalars[2 + number, 0]
+        if number < 3:
+            weight_out[number] = trust_ratio
+        else:
+            rows_out[number - 3] = trust_ratio
+        clipped = scalars[1, 0] * raws[number][...]
         tensor = tensors[number][...]
         new_first, new_second, direction = adam_direction(
             tensor, clipped, firsts[number][...], seconds[number][...], DECAYS[number]
         )
-        updated = tensor - learn_rate * scalars[2 + number : 3 + number, 0:1] * direction
+        updated = tensor - learn_rate * trust_ratio * direction
         values = [clipped, new_first, new_second, updated]
         if number < 3:
             values.append(updated.astype(BF16))
         for value in values:
             outs[at][...] = value
             at += 1
+        if number < 4:
+            for copy, after in list(zip(copies, onward))[2 * number : 2 * number + 2]:
+                copy.wait()
+                after.start()
+    for copy in onward:
+        copy.wait()
 
 
 def trust_alone(raws, state):
@@ -1188,20 +1224,27 @@
     )(*raws, *state)
 
 
-def update(scalars, raws, state):
+def update(scalars, results, raws, state):
     vmem = pl.BlockSpec(memory_space=pltpu.VMEM)
+    smem = pl.BlockSpec(memory_space=pltpu.SMEM)
+    hbm = pl.BlockSpec(memory_space=pl.ANY)
     shapes = []
     for number, tensor in enumerate(state[:5]):
         shapes += [jax.ShapeDtypeStruct(tensor.shape, F32)] * 4
         if number < 3:
             shapes.append(jax.ShapeDtypeStruct(tensor.shape, BF16))
-    return pl.pallas_call(
+    outs = pl.pallas_call(
         update_kernel,
-        out_shape=shapes,
-        in_specs=[vmem] * 21,
-        out_specs=[vmem] * len(shapes),
+        out_shape=[jax.ShapeDtypeStruct((size,), F32) for size in (1, 3, 2)]
+        + [jax.ShapeDtypeStruct(result.shape, result.dtype) for result in results]
+        + shapes,
+        in_specs=[smem, hbm, hbm] + [vmem] * 20,
+        out_specs=[smem] * 3 + [hbm] * 2 + [vmem] * len(shapes),
+        scratch_shapes=[pltpu.VMEM(result.shape, result.dtype) for result in results]
+        + [pltpu.SemaphoreType.DMA((2, 2, 4))],
         compiler_params=params(),
-    )(scalars, *raws, *state)
+    )(scalars, *results, *raws, *state)
+    return outs[:3], outs[3:5], list(outs[5:])
 
 
 def local(
@@ -1272,9 +1315,9 @@
         out_raw = lax.dynamic_slice_in_dim(out_sums, me * own_in, own_in, 1)
         raws = (reduce_part, group_part, expand_part, norm_raw, out_raw)
         scalars = trust_alone(raws, state)
-    updates = list(update(scalars, raws, state))
+    (grad_norm, weight_trust, norm_trust), results, updates = update(scalars, (block_out, input_grad), raws, state)
     updates[5:10] = [value.T for value in updates[5:10]]
-    return (block_out, input_grad, scalars[0, 0], scalars[2:5, 0], scalars[5:7, 0], *updates)
+    return (*results, grad_norm.reshape(()), weight_trust, norm_trust, *updates)
 
 
 def solution(mesh):

time: 293 us -> 275 us (0.939)
  local copies, waits for them, and re-layouts: 12.3 us -> 2.88 us
  Pallas kernels: 279 us -> 271 us
    pallas_call x1, Pallas kernels: 133 us -> 126 us  [backward(): pl.pallas_call(functools.partial(backward_kernel, images=rows // HW, owne...]
    pallas_call x1, Pallas kernels: 142 us -> 136 us  [forward(): pl.pallas_call(functools.partial(forward_kernel, images=rows // HW, gathe...]
    unnamed x5 -> x1, local copies, waits for them, and re-layouts: 6.57 us -> 0.92 us
    pallas_call x1, Pallas kernels: 3.49 us -> 8.84 us  [update(): pl.pallas_call(update_kernel, out_shape=[jax.ShapeDtypeStruct((size,), F3...]
    slice x3 -> x0, local copies, waits for them, and re-layouts: 3.8 us -> none  [the longest x1 1.3 us: local(): scalars[5:7, 0]]
where the time goes in v4:
time: 275 us
  Pallas kernels  271 us (99%)
  local copies, waits for them, and re-layouts  2.88 us (1%)
    pallas_call x1, Pallas kernels, forward(): pl.pallas_call(functools.partial(forward_kernel, images=rows // HW, gathe...  136 us
    pallas_call x1, Pallas kernels, backward(): pl.pallas_call(functools.partial(backward_kernel, images=rows // HW, owne...  126 us
    pallas_call x1, Pallas kernels, update(): pl.pallas_call(update_kernel, out_shape=[jax.ShapeDtypeStruct((size,), F3...  8.84 us

profile of v4, /device:TPU:0, one launch (start us, length us, event | category | flops | bytes accessed | tf_op | source)
XLA Modules:
  0.0 275.1 jit_solution(14075357585792385005)
XLA Ops:
  0.7 0.8 dynamic-slice_convert_fusion
  1.5 0.1 reshape.70
  1.5 0.1 copy.49
  1.6 0.1 broadcast_in_dim.7
  1.7 0.9 copy.50
  2.7 0.1 copy.51
  2.7 0.7 squeeze_reshape.3.refs_7_
  3.4 0.9 broadcast_in_dim.8.refs_2_.refs_14_
  4.4 136.1 %shard_map.393 = (bf16[784,2048]{1,0:T(8,128)(2,1)}, bf16[784,1024]{1,0:T(8,128)(2,1)}, bf16[784,1024]{1,0:T(8,128)(2,1)}, bf16[784,1024]{1,0:T(8,128)(2,1)}, bf...) custom-call(bf16[3136,512]{1,0:T(8,128)(2,1)} %refs_0_.1, ...), custom_call_target="tpu_custom_call" | custom-call | tf_op jit(solution)/shard_map/pallas_call | solution.py:620
  140.4 125.6 %shard_map.394 = (bf16[3136,512]{1,0:T(8,128)(2,1)}, bf16[3136,512]{1,0:T(8,128)(2,1)}, f32[64,1024]{1,0:T(8,128)}, f32[128,512]{1,0:T(8,128)}, f32[32,288]{1,0:...) custom-call(bf16[3136,512]{1,0:T(8,128)(2,1)} %get-tuple-element.84., ...), custom_call_target="tpu_custom_call", output_to_operand_aliasing={{0}: (0, {})} | custom-call | tf_op jit(solution)/shard_map/pallas_call | solution.py:1097
  266.1 8.8 %shard_map.395 = (f32[1]{0:T(128)}, f32[3]{0:T(128)}, f32[2]{0:T(128)}, bf16[3136,512]{1,0:T(8,128)(2,1)}, bf16[3136,512]{1,0:T(8,128)(2,1)}, /*index=5*/f32[64,...) custom-call(f32[8,128]{1,0:T(8,128)} %get-tuple-element.104.refs_0_,, ...), custom_call_target="tpu_custom_call" | custom-call | tf_op jit(solution)/shard_map/pallas_call | solution.py:1236
  (1 shorter events, 0.0 us)

commit v5 on v4

--- a/solution.py
+++ b/solution.py
@@ -275,6 +275,26 @@
             blocks[row : row + GW, 128 - left : 256 - left] = zero
 
 
+def pack_groups(transposed):
+    lanes = lax.broadcasted_iota(jnp.int32, (GW, 128), 1) - lax.broadcasted_iota(jnp.int32, (GW, 128), 0)
+    at = [dot_left(transposed, jnp.where(lanes == tap * GW, 1.0, 0.0).astype(BF16)) for tap in range(4)]
+    rows = []
+    for first in range(0, 9, 4):
+        taps = range(first, min(first + 4, 9))
+        rows.append(add_rows([at[tap % 4][tap * GW : (tap + 1) * GW] for tap in taps]))
+    return jnp.concatenate(rows, axis=0).astype(BF16)
+
+
+def spread_mask(valid, images):
+    rows = images * HW
+    image = lax.broadcasted_iota(jnp.int32, (rows, images), 0) % images
+    chosen = jnp.where(image == lax.broadcasted_iota(jnp.int32, (rows, images), 1), 1.0, 0.0)
+    frames = dot(chosen.astype(BF16), valid.astype(BF16))
+    pixel = lax.broadcasted_iota(jnp.int32, (rows, HW), 0) // images
+    own = jnp.where(pixel == lax.broadcasted_iota(jnp.int32, (rows, HW), 1), frames, 0.0)
+    return jnp.broadcast_to(jnp.sum(own, axis=1, keepdims=True), (rows, 128))
+
+
 def block_stats(z_ref, left, columns, m_ref, st_ref, step):
     rows = z_ref.shape[0]
     for part in range(0, columns, BLK):
@@ -307,9 +327,10 @@
 
 
 def forward_kernel(*refs, images, gather):
-    (feat, cotg, m_ref, np_ref, op_ref, wr_in, we_in, wg_in) = refs[:8]
+    (feat, cotg, valid_ref, np_ref, op_ref, wr_in, we_in, wg_in) = refs[:8]
     big = dict(zip(FWD_OUTS, refs[8:21]))
-    block_out, n1, n2, n3, norm_all, out_all, sums3 = refs[21:28]
+    block_out, m_ref, n1, n2, n3, norm_all, out_all, sums3 = refs[21:29]
+    refs = refs[:28] + refs[29:]
     (inner, x1, act1, slope1, x2, act2, slope2, x3, grads, wr, we, wg) = refs[28:40]
     (land_f, land_c, cot, perm, back, z1, ze, col, blocks, st1, st2, st3, st4, send, recv, moves) = refs[40:56]
     ex1, ex2, ex3, ex4 = (refs[56 + 7 * k : 63 + 7 * k] for k in range(4))
@@ -330,8 +351,8 @@
         shards = [
             links.move(wr_in, shard_r, keep=False),
             links.move(we_in, shard_e, keep=False),
-            links.move(wg_in, wg.at[here.me, here.line, here.core], keep=False),
         ]
+        wg[here.me, here.line, here.core] = pack_groups(wg_in[...].astype(BF16))
         for copy in shards:
             copy.wait()
         wr[here.me, here.line, here.core] = shard_r[...].astype(BF16)
@@ -379,6 +400,7 @@
         we_a1 = spread_out(we, here.along, upper)
     perm[...] = to_inner(rows, images)
     back[...] = to_outer(rows, images)
+    m_ref[...] = spread_mask(valid_ref[...], images)
     own_f.wait()
     for number in range(grp):
         if number:
@@ -584,7 +606,7 @@
     links.close()
 
 
-def forward(features, out_cotangent, mask, norm_params, out_params, reduce_w, expand_w, group_w, gather):
+def forward(features, out_cotangent, valid, norm_params, out_params, reduce_w, expand_w, group_w, gather):
     grp = lax.axis_size("grp")
     rows = features.shape[0] // grp
     own_in = features.shape[1]
@@ -610,7 +632,7 @@
         "we": e_shape,
         "wg": g_shape,
     }
-    small = [(3, width), (3, width), (3, channels), (4, width), (2, channels), (2, channels)]
+    small = [(rows, 128), (3, width), (3, width), (3, channels), (4, width), (2, channels), (2, channels)]
     vmem = pl.BlockSpec(memory_space=pltpu.VMEM)
     hbm = pl.BlockSpec(memory_space=pl.ANY)
     if gather:
@@ -622,7 +644,7 @@
         out_shape=[jax.ShapeDtypeStruct(shapes[name], BF16) for name in FWD_OUTS]
         + [jax.ShapeDtypeStruct(features.shape, BF16)]
         + [jax.ShapeDtypeStruct(shape, F32) for shape in small],
-        in_specs=[hbm, hbm, vmem, vmem, vmem] + [hbm] * 3,
+        in_specs=[hbm, hbm, vmem, vmem, vmem, hbm, hbm, vmem if gather else hbm],
         out_specs=[hbm] * (len(FWD_OUTS) + 1) + [vmem] * len(small),
         scratch_shapes=[pltpu.VMEM(shapes[name], BF16) for name in FWD_OUTS[:-1]]
         + [
@@ -649,7 +671,7 @@
         + sums_scratch(2, channels)
         + ([pltpu.VMEM(reduce_w.shape, F32), pltpu.VMEM(expand_w.shape, F32)] if gather else []),
         compiler_params=params(collective_id=1, has_side_effects=True),
-    )(features, out_cotangent, mask, norm_params, out_params, *weights)
+    )(features, out_cotangent, valid, norm_params, out_params, *weights)
     return dict(zip(FWD_OUTS, results)), results[len(FWD_OUTS)], results[len(FWD_OUTS) + 1 :]
 
 
@@ -1175,7 +1197,9 @@
     scalars, results = refs[0], refs[1:3]
     raws, tensors, firsts, seconds = (refs[5 * k + 3 : 5 * k + 8] for k in range(4))
     norm_out, weight_out, rows_out, *refs = refs[23:]
-    targets, outs, rooms, sems = refs[:2], refs[2:-3], refs[-3:-1], refs[-1]
+    targets, refs = refs[:2], refs[2:]
+    rooms, sems, out_sems = refs[-4:-2], refs[-2], refs[-1]
+    outs, held = refs[: len(refs) // 2 - 2], refs[len(refs) // 2 - 2 : -4]
     copies, onward = [], []
     for number, (source, room, target) in enumerate(zip(results, rooms, targets)):
         part = source.shape[0] // 4
@@ -1202,7 +1226,9 @@
         if number < 3:
             values.append(updated.astype(BF16))
         for value in values:
-            outs[at][...] = value
+            held[at][...] = value
+            onward.append(pltpu.make_async_copy(held[at], outs[at], out_sems.at[at]))
+            onward[-1].start()
             at += 1
         if number < 4:
             for copy, after in list(zip(copies, onward))[2 * number : 2 * number + 2]:
@@ -1239,9 +1265,10 @@
         + [jax.ShapeDtypeStruct(result.shape, result.dtype) for result in results]
         + shapes,
         in_specs=[smem, hbm, hbm] + [vmem] * 20,
-        out_specs=[smem] * 3 + [hbm] * 2 + [vmem] * len(shapes),
-        scratch_shapes=[pltpu.VMEM(result.shape, result.dtype) for result in results]
-        + [pltpu.SemaphoreType.DMA((2, 2, 4))],
+        out_specs=[smem] * 3 + [hbm] * (2 + len(shapes)),
+        scratch_shapes=[pltpu.VMEM(shape.shape, shape.dtype) for shape in shapes]
+        + [pltpu.VMEM(result.shape, result.dtype) for result in results]
+        + [pltpu.SemaphoreType.DMA((2, 2, 4)), pltpu.SemaphoreType.DMA((len(shapes),))],
         compiler_params=params(),
     )(scalars, *results, *raws, *state)
     return outs[:3], outs[3:5], list(outs[5:])
@@ -1275,23 +1302,20 @@
     own_in = features.shape[1]
     own_width = norm_params.shape[1]
     inside = batch == 8 and own_width == 8 * GW
-    validity = lax.dynamic_slice_in_dim(pixel_mask, me * rows, rows, 0).astype(F32)
-    mask = jnp.broadcast_to(validity.reshape(images, HW).T.reshape(rows, 1), (rows, 128))
+    valid = lax.dynamic_slice_in_dim(pixel_mask, me * rows, rows, 0).astype(F32).reshape(images, HW)
     state = (
         *(reduce_master, group_master.T, expand_master, norm_params, out_params),
         *(reduce_first, group_first.T, expand_first, norm_first, out_first),
         *(reduce_second, group_second.T, expand_second, norm_second, out_second),
     )
-    group_w = group_master.astype(BF16)
     if inside:
-        reduce_w, expand_w = reduce_master, expand_master
-        group_w = packed_groups(group_w)[0]
+        reduce_w, expand_w, group_w = reduce_master, expand_master, group_master.T
     else:
         reduce_w = lax.all_gather(reduce_master.astype(BF16), both, axis=0, tiled=True)
         expand_w = lax.all_gather(expand_master.astype(BF16), both, axis=0, tiled=True)
-        group_w = packed_groups(lax.all_gather(group_w, both, axis=1, tiled=True))
-    kept, block_out, (n1, n2, n3, norm_all, out_all, sums_three) = forward(
-        features, out_cotangent, mask, norm_params, out_params, reduce_w, expand_w, group_w, inside
+        group_w = packed_groups(lax.all_gather(group_master.astype(BF16), both, axis=1, tiled=True))
+    kept, block_out, (mask, n1, n2, n3, norm_all, out_all, sums_three) = forward(
+        features, out_cotangent, valid, norm_params, out_params, reduce_w, expand_w, group_w, inside
     )
     block_out, input_grad, reduce_part, expand_part, group_part, sums_one, sums_two, *last = backward(
         kept, block_out, mask, n1, n2, n3, norm_all, out_all, sums_three, state if inside else (), inside

time: 275 us -> 273 us (level)
  no operation moved by 1% of the time
where the time goes in v5:
time: 273 us
  Pallas kernels  270 us (99%)
    pallas_call x1, Pallas kernels, forward(): pl.pallas_call(functools.partial(forward_kernel, images=rows // HW, gathe...  136 us
    pallas_call x1, Pallas kernels, backward(): pl.pallas_call(functools.partial(backward_kernel, images=rows // HW, owne...  126 us
    pallas_call x1, Pallas kernels, update(): pl.pallas_call(update_kernel, out_shape=[jax.ShapeDtypeStruct((size,), F3...  8.67 us

profile of v5, /device:TPU:0, one launch (start us, length us, event | category | flops | bytes accessed | tf_op | source)
XLA Modules:
  0.0 272.6 jit_solution(10932843013080816850)
XLA Ops:
  0.7 0.8 dynamic-slice_convert_fusion
  1.5 0.7 reshape.62.refs_2_
  2.1 136.1 %shard_map.393 = (bf16[784,2048]{1,0:T(8,128)(2,1)}, bf16[784,1024]{1,0:T(8,128)(2,1)}, bf16[784,1024]{1,0:T(8,128)(2,1)}, bf16[784,1024]{1,0:T(8,128)(2,1)}, bf...) custom-call(bf16[3136,512]{1,0:T(8,128)(2,1)} %refs_0_.1, ...), custom_call_target="tpu_custom_call" | custom-call | tf_op jit(solution)/shard_map/pallas_call | solution.py:642
  138.2 125.5 %shard_map.394 = (bf16[3136,512]{1,0:T(8,128)(2,1)}, bf16[3136,512]{1,0:T(8,128)(2,1)}, f32[64,1024]{1,0:T(8,128)}, f32[128,512]{1,0:T(8,128)}, f32[32,288]{1,0:...) custom-call(bf16[3136,512]{1,0:T(8,128)(2,1)} %get-tuple-element.85., ...), custom_call_target="tpu_custom_call", output_to_operand_aliasing={{0}: (0, {})} | custom-call | tf_op jit(solution)/shard_map/pallas_call | solution.py:1119
  263.8 8.7 %shard_map.395 = (f32[1]{0:T(128)}, f32[3]{0:T(128)}, f32[2]{0:T(128)}, bf16[3136,512]{1,0:T(8,128)(2,1)}, bf16[3136,512]{1,0:T(8,128)(2,1)}, /*index=5*/f32[64,...) custom-call(f32[8,128]{1,0:T(8,128)} %get-tuple-element.106.refs_0_,, ...), custom_call_target="tpu_custom_call" | custom-call | tf_op jit(solution)/shard_map/pallas_call | solution.py:1262

commit v6 on v5

--- a/solution.py
+++ b/solution.py
@@ -171,7 +171,7 @@
     def __init__(self, send, recv, local):
         self.send_sems, self.recv_sems, self.local_sems = send, recv, local
         self.sent = self.moved = 0
-        self.open_sends, self.open_moves = [], []
+        self.open_sends, self.open_moves, self.at_times = [], [], []
 
     def send(self, source, target, peer, start=True):
         at = self.sent
@@ -184,6 +184,13 @@
         self.open_sends.append(copy)
         return copy
 
+    def send_when(self, condition, source, target, peer):
+        copy = self.send(source, target, peer, start=False)
+        self.open_sends.pop()
+        self.at_times.append((condition, copy))
+        pl.when(condition)(copy.start)
+        return copy
+
     def move(self, source, target, keep=True):
         copy = pltpu.make_async_copy(source, target, self.local_sems.at[self.moved])
         self.moved += 1
@@ -195,6 +202,8 @@
     def close(self):
         for copy in self.open_sends:
             copy.wait_send()
+        for condition, copy in self.at_times:
+            pl.when(condition)(copy.wait_send)
         for copy in self.open_moves:
             copy.wait()
 
@@ -390,7 +399,10 @@
     if gather:
         arrived(wr_a)
         place = wr.at[:, here.line, here.core, rest]
-        wr_l = [links.send(place, place, peer) for peer in here.along]
+        last = here.lines - 1
+        up, down = here.along[0], here.along[last - 1]
+        line_up = [links.send_when(here.line < last, place, place, up)]
+        line_down = [links.send_when(here.line > 0, place, place, down)]
         wr_b = [links.send(place, place, here.sibling)]
         arrived(wr_z)
         place = wr.at[here.me, :, here.core, head]
@@ -401,17 +413,37 @@
     perm[...] = to_inner(rows, images)
     back[...] = to_outer(rows, images)
     m_ref[...] = spread_mask(valid_ref[...], images)
-    own_f.wait()
-    for number in range(grp):
+    wr_c = []
+
+    def hand_on(steps):
+        if gather:
+            for k in steps:
+                from_below, from_above = here.line >= k, here.line <= last - k
+                pl.when(from_below)(line_up[k - 1].wait_recv)
+                place = wr.at[:, here.next_line(here.lines - k), here.core, rest]
+                if k < last:
+                    line_up.append(links.send_when(jnp.logical_and(from_below, here.line < last), place, place, up))
+                wr_c.append((from_below, links.send_when(from_below, place, place, here.sibling)))
+                pl.when(from_above)(line_down[k - 1].wait_recv)
+                place = wr.at[:, here.next_line(k), here.core, rest]
+                if k < last:
+                    line_down.append(links.send_when(jnp.logical_and(from_above, here.line > 0), place, place, down))
+                wr_c.append((from_above, links.send_when(from_above, place, place, here.sibling)))
+
+    def place_features(number):
         if number:
             from_f[number].wait_recv()
         span = aligned(here.partner(number) * own_in, own_in)
         inner[:, span] = dot(perm[...], land_f[number]).astype(BF16)
+
+    own_f.wait()
+    place_features(0)
+    hand_on(range(1, here.lines - 1))
+    for number in range(1, grp - 1):
+        place_features(number)
+    hand_on([here.lines - 1])
+    place_features(grp - 1)
     if gather:
-        for k in range(1, here.lines):
-            wr_l[k - 1].wait_recv()
-            place = wr.at[:, here.next_line(here.lines - k), here.core, rest]
-            wr_b.append(links.send(place, place, here.sibling))
         arrived(wr_g)
         place = wr.at[:, :, here.core, head]
         wr_b.append(links.send(place, place, here.sibling))
@@ -443,6 +475,8 @@
         we_z.go(1)
         we_g.go(1)
         arrived(wr_b)
+        for condition, copy in wr_c:
+            pl.when(condition)(copy.wait_recv)
     for copy in loads:
         copy.wait()
     links.move(inner, big["inner"])

time: 273 us -> 273 us (level)
  no operation moved by 1% of the time
where the time goes in v6:
time: 273 us
  Pallas kernels  270 us (99%)
    pallas_call x1, Pallas kernels, forward(): pl.pallas_call(functools.partial(forward_kernel, images=rows // HW, gathe...  135 us
    pallas_call x1, Pallas kernels, backward(): pl.pallas_call(functools.partial(backward_kernel, images=rows // HW, owne...  126 us
    pallas_call x1, Pallas kernels, update(): pl.pallas_call(update_kernel, out_shape=[jax.ShapeDtypeStruct((size,), F3...  8.67 us

profile of v6, /device:TPU:0, one launch (start us, length us, event | category | flops | bytes accessed | tf_op | source)
XLA Modules:
  0.0 272.6 jit_solution(5735347082712005595)
XLA Ops:
  0.7 0.8 dynamic-slice_convert_fusion
  1.5 0.7 reshape.62.refs_2_
  2.1 135.2 %shard_map.393 = (bf16[784,2048]{1,0:T(8,128)(2,1)}, bf16[784,1024]{1,0:T(8,128)(2,1)}, bf16[784,1024]{1,0:T(8,128)(2,1)}, bf16[784,1024]{1,0:T(8,128)(2,1)}, bf...) custom-call(bf16[3136,512]{1,0:T(8,128)(2,1)} %refs_0_.1, ...), custom_call_target="tpu_custom_call" | custom-call | tf_op jit(solution)/shard_map/pallas_call | solution.py:676
  137.3 126.4 %shard_map.394 = (bf16[3136,512]{1,0:T(8,128)(2,1)}, bf16[3136,512]{1,0:T(8,128)(2,1)}, f32[64,1024]{1,0:T(8,128)}, f32[128,512]{1,0:T(8,128)}, f32[32,288]{1,0:...) custom-call(bf16[3136,512]{1,0:T(8,128)(2,1)} %get-tuple-element.85., ...), custom_call_target="tpu_custom_call", output_to_operand_aliasing={{0}: (0, {})} | custom-call | tf_op jit(solution)/shard_map/pallas_call | solution.py:1153
  263.7 8.7 %shard_map.395 = (f32[1]{0:T(128)}, f32[3]{0:T(128)}, f32[2]{0:T(128)}, bf16[3136,512]{1,0:T(8,128)(2,1)}, bf16[3136,512]{1,0:T(8,128)(2,1)}, /*index=5*/f32[64,...) custom-call(f32[8,128]{1,0:T(8,128)} %get-tuple-element.106.refs_0_,, ...), custom_call_target="tpu_custom_call" | custom-call | tf_op jit(solution)/shard_map/pallas_call | solution.py:1296
